TPU v7x, 128 devices: a whole 4x4x4 slice. The times are simulated.
128 devices in a mesh: frame: 16 (over y, x), orbit: 8 (over z, core).
Axes of the slice: x: 4, y: 4, z: 4, core: 2. Of those that a mesh axis runs over, the one named last changes fastest.
Arguments:
- tokens: bfloat16 [65536, 1536], P(('orbit', 'frame')), parts along dimension 0, may hold values from -8 to 8
- keep_count: int32 [128], P('orbit'), parts along dimension 0, may hold values from 1 to 3, 32 in all
- keep_order: int32 [128, 4], P(('orbit', 'frame')), parts along dimension 0, may hold values from 0 to 3, each once within a row
- w_qkv: bfloat16 [1536, 4608], replicated, may hold values from -1 to 1
- w_out: bfloat16 [1536, 1536], replicated, may hold values from -0.15625 to 0.15625
Outputs:
- updated: bfloat16 [65536, 1536], P(('orbit', 'frame')), parts along dimension 0
There are 8 independent parts, one for each index of `orbit`. A program takes and returns all parts, laid end to end along the dimension named above; an argument that names none is the same for every part. Nothing has to cross between parts.
Inputs may be any that keep to these rules, and one draw needn't show every extreme that they name: `keep_count`: the counts sum to 32 and some frame keeps exactly 3 blocks. `keep_order`: each row is a permutation of the numbers 0 to 3.
All inputs are finite; a program needn't handle non-finite values.
Results may differ from a plain program's by a relative error of at most 0.0086.
Values may be sent and summed in bfloat16 or wider, within the bound.
A program may use at most 320 MiB of HBM per device.

v0:
```python
import jax
import jax.numpy as jnp
from jax import lax
from jax.sharding import PartitionSpec as P

D = 1536
HEADS = 24
HEAD_DIM = 64
BLK = 128
MOSTB = 3


def shifted(value, axis, steps):
    count = lax.axis_size(axis)
    pairs = [(source, (source + steps) % count) for source in range(count)]
    return lax.ppermute(value, axis, pairs)


def rms_rows(values):
    wide = values.astype(jnp.float32)
    return wide * lax.rsqrt(jnp.mean(wide * wide, axis=-1, keepdims=True) + 1e-06)


def frame_partial(query, keys, values, count):
    rows = query.shape[0]
    q_heads = query.reshape(rows, HEADS, HEAD_DIM)
    k_heads = keys.reshape(rows, HEADS, HEAD_DIM)
    v_heads = values.reshape(rows, HEADS, HEAD_DIM)
    scores = jnp.einsum(
        "rhd,shd->rhs", q_heads, k_heads, preferred_element_type=jnp.float32
    ) * HEAD_DIM ** (-0.5)
    live = jnp.arange(rows, dtype=jnp.int32) < count * BLK
    scores = jnp.where(live[None, None, :], scores, jnp.float32(-1e30))
    peak = jnp.max(scores, axis=-1)
    weights = jnp.exp(scores - peak[..., None])
    total = jnp.sum(weights, axis=-1)
    summed = jnp.einsum(
        "rhs,shd->rhd", weights.astype(jnp.bfloat16), v_heads, preferred_element_type=jnp.float32
    )
    return (peak, total, summed.reshape(rows, HEADS * HEAD_DIM))


def combine_all(peaks, totals, sums):
    rows = peaks.shape[1]
    top = jnp.max(peaks, axis=0)
    scale = jnp.exp(peaks - top[None])
    total = jnp.sum(scale * totals, axis=0)
    summed = jnp.sum(scale[..., None] * sums.reshape(sums.shape[0], rows, HEADS, HEAD_DIM), axis=0)
    return (summed / total[..., None]).reshape(rows, HEADS * HEAD_DIM).astype(jnp.bfloat16)


def shards(tokens, keep_count, keep_order, w_qkv, w_out):
    frames = lax.axis_size("frame")
    here = lax.axis_index("frame")
    reach = frames // 4
    width = HEADS * HEAD_DIM
    nblocks = tokens.shape[0] // BLK
    rows = MOSTB * BLK
    blocks = tokens.reshape(nblocks, BLK, D)
    order_row = keep_order[0]
    own_count = jnp.take(keep_count, here)
    kept = jnp.take(blocks, order_row[:MOSTB], axis=0).reshape(rows, D)
    normed = rms_rows(kept).astype(jnp.bfloat16)
    qkv = jnp.dot(normed, w_qkv, preferred_element_type=jnp.float32).astype(jnp.bfloat16)
    query = qkv[:, :width]
    keys = qkv[:, width : 2 * width]
    values = qkv[:, 2 * width :]
    local = frame_partial(query, keys, values, own_count)
    peak_list = [local[0]]
    total_list = [local[1]]
    sum_list = [local[2]]
    upper = (keys, values)
    lower = (keys, values)
    for step in range(1, reach + 1):
        upper = shifted((upper[0], upper[1]), "frame", 1)
        peak, total, summed = frame_partial(
            query, upper[0], upper[1], jnp.take(keep_count, (here - step) % frames)
        )
        peak_list.append(peak)
        total_list.append(total)
        sum_list.append(summed)
        lower = shifted((lower[0], lower[1]), "frame", -1)
        peak, total, summed = frame_partial(
            query, lower[0], lower[1], jnp.take(keep_count, (here + step) % frames)
        )
        peak_list.append(peak)
        total_list.append(total)
        sum_list.append(summed)
    attended = combine_all(jnp.stack(peak_list), jnp.stack(total_list), jnp.stack(sum_list))
    projected = jnp.dot(attended, w_out, preferred_element_type=jnp.float32)
    normalized = rms_rows(projected).astype(jnp.bfloat16)
    live_block = jnp.arange(MOSTB, dtype=jnp.int32) < own_count
    placing = (
        order_row[:MOSTB][None, :] == jnp.arange(nblocks, dtype=jnp.int32)[:, None]
    ) & live_block[None, :]
    placed = jnp.dot(
        placing.astype(jnp.bfloat16),
        normalized.reshape(MOSTB, BLK * D),
        preferred_element_type=jnp.float32,
    )
    return placed.astype(jnp.bfloat16).reshape(nblocks * BLK, D)


def solution(mesh):
    return jax.shard_map(
        shards,
        mesh=mesh,
        in_specs=(P(("orbit", "frame"), None), P("orbit"), P(("orbit", "frame"), None), P(), P()),
        out_specs=P(("orbit", "frame"), None),
        check_vma=False,
    )
```

profile of v0, /device:TPU:64, one launch (start us, length us, event | category | flops | bytes accessed | tf_op | source)
XLA Modules:
  0.0 358.5 jit_solution(14685750861210170563)
XLA Ops:
  2.9 11.1 %convolution_convert_fusion.1 = bf16[384,4608]{1,0:T(8,128)(2,1)S(1)} fusion(bf16[1536,4608]{1,0:T(8,128)(2,1)} %param.8, bf16[384,1536]{1,0:T(8,128)(2,1)S(1)} %bitcast_select_fusion, f32[384]{0:T(512)S(1)} %rsqrt_bitcast_fusion), kind=kOutput, calls=%fused_computation.75 | convolution fusion | flops 5439356928 | bytes 18875904 | tf_op jit(solution)/shard_map/dot_general | solution.py:64
  33.7 9.9 %bitcast_reduce_fusion.8 = (f32[384,24]{0,1:T(8,128)S(1)}, f32[24,384,384]{2,1,0:T(8,128)}) fusion(pred[384]{0:T(512)(128)(4,1)S(1)} %iota_compare_fusion.8, bf16[384,24,64]{0,2,1:T(8,128)(2,1)} %bitcast.277, bf16[384,24,64]{0,2,1:T(8,128)(2,1)S(1)} %bitcast.265), kind=kOutput, calls=%fused_computation.28 | convolution fusion | flops 463592448 | bytes 16552320 | tf_op jit(solution)/shard_map/rhd,shd->rhs/dot_general | solution.py:29
  43.7 7.9 %fusion.9 = f32[384,24]{0,1:T(8,128)S(1)} fusion(f32[24,384,384]{2,1,0:T(8,128)} %get-tuple-element.119, f32[384,24]{0,1:T(8,128)S(1)} %get-tuple-element.118, pred[384]{0:T(512)(128)(4,1)S(1)} %iota_compare_fusion.8), kind=kLoop, calls=%fused_computation.39 | loop fusion | flops 14146560 | bytes 14229888 | tf_op jit(solution)/shard_map/reduce_sum | solution.py:36
  57.6 10.2 %bitcast_dynamic-update-slice_fusion.8 = f32[9,384,24,64]{1,3,2,0:T(8,128)} fusion(bf16[384,24,64]{0,2,1:T(8,128)(2,1)} %bitcast.286, f32[24,384,384]{2,1,0:T(8,128)} %get-tuple-element.119, f32[384,24]{0,1:T(8,128)S(1)} %get-tuple-element.118, pred[384]{0:T(512)(128)(4,1)S(1)} %iota_compare_fusion.8), kind=kOutput, calls=%fused_computation.84 | convolution fusion | flops 467140608 | bytes 17731968 | tf_op jit(solution)/shard_map/rhs,shd->rhd/dot_general | solution.py:37
  70.4 10.0 %bitcast_reduce_fusion.7 = (f32[384,24]{0,1:T(8,128)S(1)}, f32[24,384,384]{2,1,0:T(8,128)}) fusion(pred[384]{0:T(512)(128)(4,1)S(1)} %iota_compare_fusion.7, bf16[384,24,64]{0,2,1:T(8,128)(2,1)} %bitcast.280, bf16[384,24,64]{0,2,1:T(8,128)(2,1)S(1)} %bitcast.266), kind=kOutput, calls=%fused_computation.25 | convolution fusion | flops 463592448 | bytes 16552320 | tf_op jit(solution)/shard_map/rhd,shd->rhs/dot_general | solution.py:29
  80.3 8.0 %fusion.11 = f32[384,24]{0,1:T(8,128)S(1)} fusion(f32[24,384,384]{2,1,0:T(8,128)} %get-tuple-element.121, f32[384,24]{0,1:T(8,128)S(1)} %get-tuple-element.120, pred[384]{0:T(512)(128)(4,1)S(1)} %iota_compare_fusion.7), kind=kLoop, calls=%fused_computation.41 | loop fusion | flops 14146560 | bytes 14229888 | tf_op jit(solution)/shard_map/reduce_sum | solution.py:36
  90.8 9.9 %bitcast_reduce_fusion.6 = (f32[384,24]{0,1:T(8,128)S(1)}, f32[24,384,384]{2,1,0:T(8,128)}) fusion(pred[384]{0:T(512)(128)(4,1)S(1)} %iota_compare_fusion.6, bf16[384,24,64]{0,2,1:T(8,128)(2,1)} %bitcast.281, bf16[384,24,64]{0,2,1:T(8,128)(2,1)S(1)} %bitcast.267), kind=kOutput, calls=%fused_computation.22 | convolution fusion | flops 463592448 | bytes 16552320 | tf_op jit(solution)/shard_map/rhd,shd->rhs/dot_general | solution.py:29
  106.5 8.0 %fusion.13 = f32[384,24]{0,1:T(8,128)S(1)} fusion(f32[24,384,384]{2,1,0:T(8,128)} %get-tuple-element.123, f32[384,24]{0,1:T(8,128)S(1)} %get-tuple-element.122, pred[384]{0:T(512)(128)(4,1)S(1)} %iota_compare_fusion.6), kind=kLoop, calls=%fused_computation.43 | loop fusion | flops 14146560 | bytes 14229888 | tf_op jit(solution)/shard_map/reduce_sum | solution.py:36
  116.9 10.2 %bitcast_dynamic-update-slice_fusion.7 = f32[9,384,24,64]{1,3,2,0:T(8,128)} fusion(f32[9,384,24,64]{1,3,2,0:T(8,128)} %bitcast_dynamic-update-slice_fusion.8, bf16[384,24,64]{0,2,1:T(8,128)(2,1)} %bitcast.287, f32[24,384,384]{2,1,0:T(8,128)} %get-tuple-element.121, f32[384,24]{0,1:T(8,128)S(1)} %get-tuple-element.120, pred[384]{0:T(512)(128)(4,1)S(1)} %iota_compare_fusion.7), kind=kOutput, calls=%fused_computation.83 | convolution fusion | flops 467140608 | bytes 17731968 | tf_op jit(solution)/shard_map/rhs,shd->rhd/dot_general | solution.py:37
  134.4 9.8 %bitcast_dynamic-update-slice_fusion.6 = f32[9,384,24,64]{1,3,2,0:T(8,128)} fusion(f32[9,384,24,64]{1,3,2,0:T(8,128)} %bitcast_dynamic-update-slice_fusion.7, bf16[384,24,64]{0,2,1:T(8,128)(2,1)S(1)} %bitcast.288, f32[24,384,384]{2,1,0:T(8,128)} %get-tuple-element.123, f32[384,24]{0,1:T(8,128)S(1)} %get-tuple-element.122, ...), kind=kOutput, calls=%fused_computation.82 | convolution fusion | flops 467140608 | bytes 17731968 | tf_op jit(solution)/shard_map/rhs,shd->rhd/dot_general | solution.py:37
  152.8 8.0 %fusion.15 = f32[384,24]{0,1:T(8,128)S(1)} fusion(f32[24,384,384]{2,1,0:T(8,128)} %get-tuple-element.125, f32[384,24]{0,1:T(8,128)S(1)} %get-tuple-element.124, pred[384]{0:T(512)(128)(4,1)S(1)} %iota_compare_fusion.5), kind=kLoop, calls=%fused_computation.45 | loop fusion | flops 14146560 | bytes 14229888 | tf_op jit(solution)/shard_map/reduce_sum | solution.py:36
  174.9 7.9 %fusion.17 = f32[384,24]{0,1:T(8,128)S(1)} fusion(f32[24,384,384]{2,1,0:T(8,128)} %get-tuple-element.127, f32[384,24]{0,1:T(8,128)S(1)} %get-tuple-element.126, pred[384]{0:T(512)(128)(4,1)S(1)} %iota_compare_fusion.4), kind=kLoop, calls=%fused_computation.47 | loop fusion | flops 14146560 | bytes 14229888 | tf_op jit(solution)/shard_map/reduce_sum | solution.py:36
  184.7 9.9 %bitcast_dynamic-update-slice_fusion.5 = f32[9,384,24,64]{1,3,2,0:T(8,128)} fusion(f32[9,384,24,64]{1,3,2,0:T(8,128)} %bitcast_dynamic-update-slice_fusion.6, bf16[384,24,64]{0,2,1:T(8,128)(2,1)S(1)} %bitcast.289, f32[24,384,384]{2,1,0:T(8,128)} %get-tuple-element.125, f32[384,24]{0,1:T(8,128)S(1)} %get-tuple-element.124, ...), kind=kOutput, calls=%fused_computation.81 | convolution fusion | flops 467140608 | bytes 17731968 | tf_op jit(solution)/shard_map/rhs,shd->rhd/dot_general | solution.py:37
  202.0 9.8 %bitcast_dynamic-update-slice_fusion.4 = f32[9,384,24,64]{1,3,2,0:T(8,128)} fusion(f32[9,384,24,64]{1,3,2,0:T(8,128)} %bitcast_dynamic-update-slice_fusion.5, bf16[384,24,64]{0,2,1:T(8,128)(2,1)S(1)} %bitcast.290, f32[24,384,384]{2,1,0:T(8,128)} %get-tuple-element.127, f32[384,24]{0,1:T(8,128)S(1)} %get-tuple-element.126, ...), kind=kOutput, calls=%fused_computation.80 | convolution fusion | flops 467140608 | bytes 17731968 | tf_op jit(solution)/shard_map/rhs,shd->rhd/dot_general | solution.py:37
  213.5 6.8 %bitcast_reduce_fusion.3 = (f32[384,24]{0,1:T(8,128)S(1)}, f32[24,384,384]{2,1,0:T(8,128)}) fusion(pred[384]{0:T(512)(128)(4,1)S(1)} %iota_compare_fusion.3, bf16[384,24,64]{0,2,1:T(8,128)(2,1)S(1)} %bitcast.284, bf16[384,24,64]{0,2,1:T(8,128)(2,1)S(1)} %bitcast.270), kind=kOutput, calls=%fused_computation.13 | convolution fusion | flops 463592448 | bytes 16552320 | tf_op jit(solution)/shard_map/rhd,shd->rhs/dot_general | solution.py:29
  220.4 8.0 %fusion.19 = f32[384,24]{0,1:T(8,128)S(1)} fusion(f32[24,384,384]{2,1,0:T(8,128)} %get-tuple-element.129, f32[384,24]{0,1:T(8,128)S(1)} %get-tuple-element.128, pred[384]{0:T(512)(128)(4,1)S(1)} %iota_compare_fusion.3), kind=kLoop, calls=%fused_computation.49 | loop fusion | flops 14146560 | bytes 14229888 | tf_op jit(solution)/shard_map/reduce_sum | solution.py:36
  242.4 8.0 %fusion.21 = f32[384,24]{0,1:T(8,128)S(1)} fusion(f32[24,384,384]{2,1,0:T(8,128)} %get-tuple-element.131, f32[384,24]{0,1:T(8,128)S(1)} %get-tuple-element.130, pred[384]{0:T(512)(128)(4,1)S(1)} %iota_compare_fusion.2), kind=kLoop, calls=%fused_computation.51 | loop fusion | flops 14146560 | bytes 14229888 | tf_op jit(solution)/shard_map/reduce_sum | solution.py:36
  252.3 9.9 %bitcast_dynamic-update-slice_fusion.3 = f32[9,384,24,64]{1,3,2,0:T(8,128)} fusion(f32[9,384,24,64]{1,3,2,0:T(8,128)} %bitcast_dynamic-update-slice_fusion.4, bf16[384,24,64]{0,2,1:T(8,128)(2,1)S(1)} %bitcast.291, f32[24,384,384]{2,1,0:T(8,128)} %get-tuple-element.129, f32[384,24]{0,1:T(8,128)S(1)} %get-tuple-element.128, ...), kind=kOutput, calls=%fused_computation.79 | convolution fusion | flops 467140608 | bytes 17731968 | tf_op jit(solution)/shard_map/rhs,shd->rhd/dot_general | solution.py:37
  269.3 9.8 %bitcast_dynamic-update-slice_fusion.2 = f32[9,384,24,64]{1,3,2,0:T(8,128)} fusion(f32[9,384,24,64]{1,3,2,0:T(8,128)} %bitcast_dynamic-update-slice_fusion.3, bf16[384,24,64]{0,2,1:T(8,128)(2,1)S(1)} %bitcast.292, f32[24,384,384]{2,1,0:T(8,128)} %get-tuple-element.131, f32[384,24]{0,1:T(8,128)S(1)} %get-tuple-element.130, ...), kind=kOutput, calls=%fused_computation.78 | convolution fusion | flops 467140608 | bytes 17731968 | tf_op jit(solution)/shard_map/rhs,shd->rhd/dot_general | solution.py:37
  287.8 7.9 %fusion.23 = f32[384,24]{0,1:T(8,128)S(1)} fusion(f32[24,384,384]{2,1,0:T(8,128)} %get-tuple-element.133, f32[384,24]{0,1:T(8,128)S(1)} %get-tuple-element.132, pred[384]{0:T(512)(128)(4,1)S(1)} %iota_compare_fusion.1), kind=kLoop, calls=%fused_computation.53 | loop fusion | flops 14146560 | bytes 14229888 | tf_op jit(solution)/shard_map/reduce_sum | solution.py:36
  304.4 8.0 %fusion.25 = f32[384,24]{0,1:T(8,128)S(1)} fusion(f32[24,384,384]{2,1,0:T(8,128)} %get-tuple-element.135, f32[384,24]{0,1:T(8,128)S(1)} %get-tuple-element.134, pred[384]{0:T(512)(128)(4,1)S(1)} %iota_compare_fusion), kind=kLoop, calls=%fused_computation.55 | loop fusion | flops 14146560 | bytes 14229888 | tf_op jit(solution)/shard_map/reduce_sum | solution.py:36
  314.4 9.8 %bitcast_dynamic-update-slice_fusion.1 = f32[9,384,24,64]{1,3,2,0:T(8,128)} fusion(f32[9,384,24,64]{1,3,2,0:T(8,128)} %bitcast_dynamic-update-slice_fusion.2, bf16[384,24,64]{0,2,1:T(8,128)(2,1)S(1)} %bitcast.293, f32[24,384,384]{2,1,0:T(8,128)} %get-tuple-element.133, f32[384,24]{0,1:T(8,128)S(1)} %get-tuple-element.132, ...), kind=kOutput, calls=%fused_computation.77 | convolution fusion | flops 467140608 | bytes 17731968 | tf_op jit(solution)/shard_map/rhs,shd->rhd/dot_general | solution.py:37
  325.9 9.8 %bitcast_dynamic-update-slice_fusion = f32[9,384,24,64]{1,3,2,0:T(8,128)} fusion(f32[9,384,24,64]{1,3,2,0:T(8,128)} %bitcast_dynamic-update-slice_fusion.1, bf16[384,24,64]{0,2,1:T(8,128)(2,1)S(1)} %bitcast.294, f32[24,384,384]{2,1,0:T(8,128)} %get-tuple-element.135, f32[384,24]{0,1:T(8,128)S(1)} %get-tuple-element.134, pred[384]{0:T(512)(128)(4,1)S(1)} %iota_compare_fusion), kind=kOutput, calls=%fused_computation.76 | convolution fusion | flops 467140608 | bytes 17731968 | tf_op jit(solution)/shard_map/rhs,shd->rhd/dot_general | solution.py:37
  335.8 10.3 %multiply_reduce_fusion = f32[384,24,64]{0,2,1:T(8,128)S(1)} fusion(f32[9,384,24,64]{1,3,2,0:T(8,128)} %bitcast_dynamic-update-slice_fusion, f32[9,384,24]{1,2,0:T(8,128)S(1)} %get-tuple-element.105), kind=kLoop, calls=%fused_computation.2 | loop fusion | flops 10027008 | bytes 23924736 | tf_op jit(solution)/shard_map/reduce_sum | solution.py:48
  (120 shorter events, 132.6 us)
Async XLA Ops:
  0.0 1.5 copy-start
  2.9 26.1 %copy-start.5 = (s32[1,4]{1,0:T(1,128)S(1)}, s32[1,4]{1,0:T(1,128)}, u32[]{:S(2)}) copy-start(s32[1,4]{1,0:T(1,128)} %param.7) | copy-start | bytes 52
  2.9 26.6 %copy-start.2 = (s32[16]{0:T(128)S(1)}, s32[16]{0:T(128)}, u32[]{:S(2)}) copy-start(s32[16]{0:T(128)} %param.6) | copy-start | bytes 196
  15.7 52.1 %collective-permute-start = (bf16[384,1536]{1,0:T(8,128)(2,1)}, bf16[384,1536]{1,0:T(8,128)(2,1)}, u32[]{:S(2)}, u32[]{:S(2)}) collective-permute-start(bf16[384,1536]{1,0:T(8,128)(2,1)} %get-tuple-element.108), channel_id=1, source_target_pairs={{0,8},{8,16},{16,24},{24,32},{32,40},{40,48},{48,56},{56,64},{64,7... | collective-permute-start | bytes 3538952 | tf_op jit(solution)/shard_map/ppermute | solution.py:16
  17.2 71.2 %collective-permute-start.1 = (bf16[384,1536]{1,0:T(8,128)(2,1)}, bf16[384,1536]{1,0:T(8,128)(2,1)}, u32[]{:S(2)}, u32[]{:S(2)}) collective-permute-start(bf16[384,1536]{1,0:T(8,128)(2,1)} %get-tuple-element.108), channel_id=1, source_target_pairs={{0,120},{8,0},{16,8},{24,16},{32,24},{40,32},{48,40},{56,48},{64,5... | collective-permute-start | bytes 3538952 | tf_op jit(solution)/shard_map/ppermute | solution.py:16
  21.0 93.5 %collective-permute-start.8 = (bf16[384,1536]{1,0:T(8,128)(2,1)S(1)}, bf16[384,1536]{1,0:T(8,128)(2,1)}, u32[]{:S(2)}, u32[]{:S(2)}) collective-permute-start(bf16[384,1536]{1,0:T(8,128)(2,1)S(1)} %get-tuple-element.107), channel_id=1, source_target_pairs={{0,8},{8,16},{16,24},{24,32},{32,40},{40,48},{48,56},{56,64},{64,7... | collective-permute-start | bytes 3538952 | tf_op jit(solution)/shard_map/ppermute | solution.py:16
  21.0 106.1 %collective-permute-start.9 = (bf16[384,1536]{1,0:T(8,128)(2,1)S(1)}, bf16[384,1536]{1,0:T(8,128)(2,1)}, u32[]{:S(2)}, u32[]{:S(2)}) collective-permute-start(bf16[384,1536]{1,0:T(8,128)(2,1)S(1)} %get-tuple-element.107), channel_id=1, source_target_pairs={{0,120},{8,0},{16,8},{24,16},{32,24},{40,32},{48,40},{56,48},{64,5... | collective-permute-start | bytes 3538952 | tf_op jit(solution)/shard_map/ppermute | solution.py:16
  100.7 43.5 %collective-permute-start.2 = (bf16[384,1536]{1,0:T(8,128)(2,1)}, bf16[384,1536]{1,0:T(8,128)(2,1)}, u32[]{:S(2)}, u32[]{:S(2)}) collective-permute-start(bf16[384,1536]{1,0:T(8,128)(2,1)} %collective-permute-done), channel_id=1, source_target_pairs={{0,8},{8,16},{16,24},{24,32},{32,40},{40,48},{48,56},{56,64},{64,7... | collective-permute-start | bytes 3538952 | tf_op jit(solution)/shard_map/ppermute | solution.py:16
  100.7 60.1 %collective-permute-start.3 = (bf16[384,1536]{1,0:T(8,128)(2,1)}, bf16[384,1536]{1,0:T(8,128)(2,1)}, u32[]{:S(2)}, u32[]{:S(2)}) collective-permute-start(bf16[384,1536]{1,0:T(8,128)(2,1)} %collective-permute-done.1), channel_id=1, source_target_pairs={{0,120},{8,0},{16,8},{24,16},{32,24},{40,32},{48,40},{56,48},{64,5... | collective-permute-start | bytes 3538952 | tf_op jit(solution)/shard_map/ppermute | solution.py:16
  116.9 65.9 %collective-permute-start.10 = (bf16[384,1536]{1,0:T(8,128)(2,1)}, bf16[384,1536]{1,0:T(8,128)(2,1)}, u32[]{:S(2)}, u32[]{:S(2)}) collective-permute-start(bf16[384,1536]{1,0:T(8,128)(2,1)} %collective-permute-done.8), channel_id=1, source_target_pairs={{0,8},{8,16},{16,24},{24,32},{32,40},{40,48},{48,56},{56,64},{64,7... | collective-permute-start | bytes 3538952 | tf_op jit(solution)/shard_map/ppermute | solution.py:16
  128.8 65.7 %collective-permute-start.11 = (bf16[384,1536]{1,0:T(8,128)(2,1)}, bf16[384,1536]{1,0:T(8,128)(2,1)}, u32[]{:S(2)}, u32[]{:S(2)}) collective-permute-start(bf16[384,1536]{1,0:T(8,128)(2,1)} %collective-permute-done.9), channel_id=1, source_target_pairs={{0,120},{8,0},{16,8},{24,16},{32,24},{40,32},{48,40},{56,48},{64,5... | collective-permute-start | bytes 3538952 | tf_op jit(solution)/shard_map/ppermute | solution.py:16
  169.3 42.5 %collective-permute-start.4 = (bf16[384,1536]{1,0:T(8,128)(2,1)}, bf16[384,1536]{1,0:T(8,128)(2,1)}, u32[]{:S(2)}, u32[]{:S(2)}) collective-permute-start(bf16[384,1536]{1,0:T(8,128)(2,1)} %collective-permute-done.2), channel_id=1, source_target_pairs={{0,8},{8,16},{16,24},{24,32},{32,40},{40,48},{48,56},{56,64},{64,7... | collective-permute-start | bytes 3538952 | tf_op jit(solution)/shard_map/ppermute | solution.py:16
  169.3 59.1 %collective-permute-start.5 = (bf16[384,1536]{1,0:T(8,128)(2,1)}, bf16[384,1536]{1,0:T(8,128)(2,1)}, u32[]{:S(2)}, u32[]{:S(2)}) collective-permute-start(bf16[384,1536]{1,0:T(8,128)(2,1)} %collective-permute-done.3), channel_id=1, source_target_pairs={{0,120},{8,0},{16,8},{24,16},{32,24},{40,32},{48,40},{56,48},{64,5... | collective-permute-start | bytes 3538952 | tf_op jit(solution)/shard_map/ppermute | solution.py:16
  184.6 65.9 %collective-permute-start.12 = (bf16[384,1536]{1,0:T(8,128)(2,1)}, bf16[384,1536]{1,0:T(8,128)(2,1)}, u32[]{:S(2)}, u32[]{:S(2)}) collective-permute-start(bf16[384,1536]{1,0:T(8,128)(2,1)} %collective-permute-done.10), channel_id=1, source_target_pairs={{0,8},{8,16},{16,24},{24,32},{32,40},{40,48},{48,56},{56,64},{64,7... | collective-permute-start | bytes 3538952 | tf_op jit(solution)/shard_map/ppermute | solution.py:16
  196.2 66.0 %collective-permute-start.13 = (bf16[384,1536]{1,0:T(8,128)(2,1)}, bf16[384,1536]{1,0:T(8,128)(2,1)}, u32[]{:S(2)}, u32[]{:S(2)}) collective-permute-start(bf16[384,1536]{1,0:T(8,128)(2,1)} %collective-permute-done.11), channel_id=1, source_target_pairs={{0,120},{8,0},{16,8},{24,16},{32,24},{40,32},{48,40},{56,48},{64,5... | collective-permute-start | bytes 3538952 | tf_op jit(solution)/shard_map/ppermute | solution.py:16
  236.9 42.2 %collective-permute-start.6 = (bf16[384,1536]{1,0:T(8,128)(2,1)}, bf16[384,1536]{1,0:T(8,128)(2,1)}, u32[]{:S(2)}, u32[]{:S(2)}) collective-permute-start(bf16[384,1536]{1,0:T(8,128)(2,1)} %collective-permute-done.4), channel_id=1, source_target_pairs={{0,8},{8,16},{16,24},{24,32},{32,40},{40,48},{48,56},{56,64},{64,7... | collective-permute-start | bytes 3538952 | tf_op jit(solution)/shard_map/ppermute | solution.py:16
  236.9 58.8 %collective-permute-start.7 = (bf16[384,1536]{1,0:T(8,128)(2,1)}, bf16[384,1536]{1,0:T(8,128)(2,1)}, u32[]{:S(2)}, u32[]{:S(2)}) collective-permute-start(bf16[384,1536]{1,0:T(8,128)(2,1)} %collective-permute-done.5), channel_id=1, source_target_pairs={{0,120},{8,0},{16,8},{24,16},{32,24},{40,32},{48,40},{56,48},{64,5... | collective-permute-start | bytes 3538952 | tf_op jit(solution)/shard_map/ppermute | solution.py:16
  252.2 60.2 %collective-permute-start.14 = (bf16[384,1536]{1,0:T(8,128)(2,1)}, bf16[384,1536]{1,0:T(8,128)(2,1)}, u32[]{:S(2)}, u32[]{:S(2)}) collective-permute-start(bf16[384,1536]{1,0:T(8,128)(2,1)} %collective-permute-done.12), channel_id=1, source_target_pairs={{0,8},{8,16},{16,24},{24,32},{32,40},{40,48},{48,56},{56,64},{64,7... | collective-permute-start | bytes 3538952 | tf_op jit(solution)/shard_map/ppermute | solution.py:16
  263.9 60.3 %collective-permute-start.15 = (bf16[384,1536]{1,0:T(8,128)(2,1)}, bf16[384,1536]{1,0:T(8,128)(2,1)}, u32[]{:S(2)}, u32[]{:S(2)}) collective-permute-start(bf16[384,1536]{1,0:T(8,128)(2,1)} %collective-permute-done.13), channel_id=1, source_target_pairs={{0,120},{8,0},{16,8},{24,16},{32,24},{40,32},{48,40},{56,48},{64,5... | collective-permute-start | bytes 3538952 | tf_op jit(solution)/shard_map/ppermute | solution.py:16
  335.7 10.7 %slice-start = ((s8[4718592]{0:T(1024)(128)(4,1)}), s8[4194304]{0:T(1024)(128)(4,1)S(1)}, s32[]{:S(2)}) async-start(s8[4718592]{0:T(1024)(128)(4,1)} %bitcast.274), calls=%async_computation | async-start | bytes 8388608
  335.8 10.6 %slice-start.1 = ((s8[4718592]{0:T(1024)(128)(4,1)}), s8[524288]{0:T(1024)(128)(4,1)S(1)}, s32[]{:S(2)}) async-start(s8[4718592]{0:T(1024)(128)(4,1)} %bitcast.274), calls=%async_computation.1 | async-start | bytes 1048576
  346.1 5.8 %copy-start.3 = (s32[3]{0:T(128)S(1)}, s32[3]{0:T(128)}, u32[]{:S(2)}) copy-start(s32[3]{0:T(128)} %slice_bitcast_fusion) | copy-start | bytes 40
  346.1 5.8 %copy-start.4 = (pred[3]{0:T(512)(128)(4,1)S(1)}, pred[3]{0:T(512)(128)(4,1)}, u32[]{:S(2)}) copy-start(pred[3]{0:T(512)(128)(4,1)} %iota_compare_fusion.10) | copy-start | bytes 13
  346.1 11.8 %copy-start.1 = (bf16[512,1536]{1,0:T(8,128)(2,1)S(1)}, bf16[512,1536]{1,0:T(8,128)(2,1)}, u32[]{:S(2)}) copy-start(bf16[512,1536]{1,0:T(8,128)(2,1)} %param.5) | copy-start | bytes 4718596
where the time goes:
time: 364 us; the launch traced here: 358 us
  matrix products  175 us (48%)
  other arithmetic  86.6 us (24%)
  local copies, waits for them, and re-layouts  45.1 us (12%)
  starting transfers between devices  44.6 us (12%)
  between operations  6.78 us (2%)
    dot_general x9, matrix products, frame_partial(): jnp.einsum('rhs,shd->rhd', weights.astype(jnp.bfloat16), v_heads, preferr...  89.1 us
    reduce_sum x9, other arithmetic, frame_partial(): total = jnp.sum(weights, axis=-1)  71.9 us
    dot_general x9, matrix products, frame_partial(): jnp.einsum('rhd,shd->rhs', q_heads, k_heads, preferred_element_type=jnp.f...  70.8 us
    ppermute x16, starting transfers between devices, shifted(): return lax.ppermute(value, axis, pairs)  44.6 us
    ppermute x16, local copies, waits for them, and re-layouts, shifted(): return lax.ppermute(value, axis, pairs)  29.9 us
    dot_general x1, matrix products, shards(): jnp.dot(normed, w_qkv, preferred_element_type=jnp.float32)  11.1 us
    reduce_sum x1, other arithmetic, combine_all(): jnp.sum(scale[..., None] * sums.reshape(sums.shape[0], rows, HEADS, HEAD_...  10.3 us
  transfers between devices with their start and end apart: 16, of which 0 were waited for; matrix products, arithmetic and copies ran while one was open for 72% of the time, Pallas kernels for 0%

commit v1 on v0

v1 whole, which is shorter than its diff:
```python
import functools

import jax
import jax.numpy as jnp
from jax import lax
from jax.experimental import pallas as pl
from jax.experimental.pallas import tpu as pltpu
from jax.sharding import PartitionSpec as P

D = 1536
HEADS = 24
HEAD_DIM = 64
BLK = 128
MOSTB = 3
ROWS = MOSTB * BLK
SIDE = 4
GW = 384
PAIRS = 3
CH = 512
NCH = 7
KROWS = 36 * BLK + CH
SCALE = HEAD_DIM ** (-0.5) * 1.4426950408889634
VMEM = 60 * 2**20
MESH = pl.DeviceIdType.MESH


def place():
    me = lax.axis_index("frame")
    return me // SIDE, me % SIDE


def device(y, x):
    return {"frame": (y % SIDE) * SIDE + x % SIDE}


def norm_kernel(order, tok, out):
    wide = tok[...].astype(jnp.float32)
    scale = lax.rsqrt(jnp.mean(wide * wide, axis=-1, keepdims=True) + 1e-06)
    out[...] = (wide * scale).astype(jnp.bfloat16)


def norm_kept(order_row, tokens):
    return pl.pallas_call(
        norm_kernel,
        grid_spec=pltpu.PrefetchScalarGridSpec(
            num_scalar_prefetch=1,
            grid=(MOSTB,),
            in_specs=[pl.BlockSpec((BLK, D), lambda j, order: (order[j], 0))],
            out_specs=pl.BlockSpec((BLK, D), lambda j, order: (j, 0)),
        ),
        out_shape=jax.ShapeDtypeStruct((ROWS, D), jnp.bfloat16),
        name="norm_kept",
    )(order_row, tokens)


BLOCKS = ((0, 1), (0, 2), (1, 1), (1, 2), (3, 1), (3, 2), (2, 1), (2, 2), (1, 0), (3, 0), (2, 0), (0, 0))


def exchange_kernel(normed, w, kv, q, wbuf, kvs, qs, wsem, xs, xr, qss, qsr, ys, yr):
    y, x = place()
    loads = []
    for i, (delta, kind) in enumerate(BLOCKS):
        col = pl.multiple_of(kind * (HEADS * HEAD_DIM) + ((x + delta) % SIDE) * GW, 128)
        load = pltpu.make_async_copy(w.at[:, pl.ds(col, GW)], wbuf.at[i], wsem.at[i])
        load.start()
        loads.append(load)
    barrier = pltpu.get_barrier_semaphore()
    peers = [(0, 1), (0, 2), (0, 3), (1, 0), (3, 0)]
    for dy, dx in peers:
        pl.semaphore_signal(barrier, inc=1, device_id=device(y + dy, x + dx), device_id_type=MESH)
    pl.semaphore_wait(barrier, len(peers))

    def product(i, put):
        loads[i].wait()

        def rows(r, carry):
            at = pl.ds(pl.multiple_of(r * BLK, BLK), BLK)
            value = jnp.dot(normed[at, :], wbuf[i], preferred_element_type=jnp.float32)
            put(at, value)
            return carry

        lax.fori_loop(0, MOSTB, rows, 0)

    def up_down(delta):
        frame = (x - delta) % SIDE
        copies = []
        for way, (dy, base) in enumerate(((1, 0), (-1, 2 * SIDE))):
            copy = pltpu.make_async_remote_copy(
                kv.at[SIDE + frame],
                kv.at[base + frame],
                ys.at[way, delta],
                yr.at[way, delta],
                device_id=device(y + dy, x),
                device_id_type=MESH,
            )
            copy.start()
            copies.append(copy)
        return copies

    sent = []
    across = {}
    for i, (delta, kind) in enumerate(BLOCKS):
        if kind == 0:

            def put(at, value, delta=delta):
                value = (value * SCALE).astype(jnp.bfloat16)
                if delta == 0:
                    q[x, at, :] = value
                else:
                    qs[delta, at, :] = value
        else:

            def put(at, value, delta=delta, kind=kind):
                cols = pl.ds((kind - 1) * GW, GW)
                if delta == 0:
                    kv[SIDE + x, at, cols] = value.astype(jnp.bfloat16)
                else:
                    kvs[delta, at, cols] = value.astype(jnp.bfloat16)

        product(i, put)
        if delta == 0 and kind == 2:
            sent += up_down(0)
        if delta and kind == 2:
            across[delta] = pltpu.make_async_remote_copy(
                kvs.at[delta], kv.at[SIDE + x], xs.at[delta], xr.at[delta],
                device_id=device(y, x + delta), device_id_type=MESH,
            )
            across[delta].start()
        if delta and kind == 0:
            copy = pltpu.make_async_remote_copy(
                qs.at[delta], q.at[x], qss.at[delta], qsr.at[delta],
                device_id=device(y, x + delta), device_id_type=MESH,
            )
            copy.start()
            sent.append(copy)
    for delta in (1, 3, 2):
        across[delta].wait()
        sent += up_down(delta)
    for copy in sent:
        copy.wait()


def exchange(normed, w_qkv):
    dma = pltpu.SemaphoreType.DMA
    vmem = pl.BlockSpec(memory_space=pltpu.VMEM)
    return pl.pallas_call(
        exchange_kernel,
        out_shape=(
            jax.ShapeDtypeStruct((3 * SIDE, ROWS, 2 * GW), jnp.bfloat16),
            jax.ShapeDtypeStruct((SIDE, ROWS, GW), jnp.bfloat16),
        ),
        in_specs=[vmem, pl.BlockSpec(memory_space=pl.ANY)],
        out_specs=(vmem, vmem),
        scratch_shapes=[
            pltpu.VMEM((len(BLOCKS), D, GW), jnp.bfloat16),
            pltpu.VMEM((SIDE, ROWS, 2 * GW), jnp.bfloat16),
            pltpu.VMEM((SIDE, ROWS, GW), jnp.bfloat16),
            dma((len(BLOCKS),)),
            dma((SIDE,)),
            dma((SIDE,)),
            dma((SIDE,)),
            dma((SIDE,)),
            dma((2, SIDE)),
            dma((2, SIDE)),
        ],
        compiler_params=pltpu.CompilerParams(
            collective_id=0, has_side_effects=True, vmem_limit_bytes=VMEM
        ),
        name="exchange",
    )(normed, w_qkv)


def attend_kernel(counts, q, kv, out, keys, vals, masked, s0, s1, m0, m1, acc):
    low = lax.broadcasted_iota(jnp.int32, (1, 128), 1) < HEAD_DIM
    one = jnp.ones((BLK, 128), jnp.bfloat16)

    def pack(slot, at):
        frame, block = slot // MOSTB, slot % MOSTB
        live = block < counts[frame]

        @pl.when(live)
        def _():
            rows = pl.ds(pl.multiple_of(block * BLK, BLK), BLK)
            to = pl.ds(pl.multiple_of(at * BLK, BLK), BLK)
            for c in range(PAIRS):
                cols = slice(c * 128, (c + 1) * 128)
                keys[c, to, :] = kv[frame, rows, cols]
                v = kv[frame, rows, GW + c * 128 : GW + (c + 1) * 128]
                vals[c, 0, to, :] = jnp.where(low, v, one)
                vals[c, 1, to, :] = jnp.where(low, one, v)

        return at + live.astype(jnp.int32)

    total = lax.fori_loop(0, 3 * SIDE * MOSTB, pack, 0)
    tail = pl.ds(pl.multiple_of(total * BLK, BLK), CH)
    for c in range(PAIRS):
        keys[c, tail, :] = jnp.zeros((CH, 128), jnp.bfloat16)
        for h in range(2):
            vals[c, h, tail, :] = jnp.zeros((CH, 128), jnp.bfloat16)

    def frame_rows(f, first, blocks, rows):
        chunks = pl.cdiv(blocks, CH // BLK)
        limit = blocks * BLK
        for c in range(PAIRS):
            value = q[f, 0:rows, c * 128 : (c + 1) * 128]
            zero = jnp.zeros_like(value)
            masked[2 * c, 0:rows, :] = jnp.where(low, value, zero)
            masked[2 * c + 1, 0:rows, :] = jnp.where(low, zero, value)

        def score(head, j, s, m):
            at = pl.ds(pl.multiple_of(first * BLK + j * CH, BLK), CH)
            value = lax.dot_general(
                masked[head, 0:rows, :], keys[head // 2, at, :],
                (((1,), (1,)), ((), ())), preferred_element_type=jnp.float32,
            )
            col = lax.broadcasted_iota(jnp.int32, (1, CH), 1) + j * CH
            value = jnp.where(col < limit, value, -1e30)
            s[j, 0:rows, :] = value
            top = m[0:rows, :]
            for t in range(CH // 128):
                top = jnp.maximum(top, value[:, t * 128 : (t + 1) * 128])
            m[0:rows, :] = top

        def begin(m):
            m[0:rows, :] = jnp.full((rows, 128), -1e30, jnp.float32)

        def settle(m):
            m[0:rows, :] = jnp.broadcast_to(
                jnp.max(m[0:rows, :], axis=1, keepdims=True), (rows, 128)
            )

        def weigh(head, j, s, m):
            at = pl.ds(pl.multiple_of(first * BLK + j * CH, BLK), CH)
            top = m[0:rows, :]
            value = s[j, 0:rows, :]
            p = jnp.exp2(value - jnp.concatenate([top] * (CH // 128), axis=1)).astype(jnp.bfloat16)
            acc[0:rows, :] += jnp.dot(
                p, vals[head // 2, head % 2, at, :], preferred_element_type=jnp.float32
            )

        def finish(head):
            value = acc[0:rows, :]
            ratio = value / pltpu.roll(value, HEAD_DIM, 1)
            cols = slice((head // 2) * 128, (head // 2 + 1) * 128)
            if head % 2 == 0:
                out[f, 0:rows, cols] = ratio.astype(jnp.bfloat16)
            else:
                before = out[f, 0:rows, cols]
                out[f, 0:rows, cols] = jnp.where(low, before, ratio.astype(jnp.bfloat16))

        bufs = ((s0, m0), (s1, m1))
        begin(m0)
        lax.fori_loop(0, chunks, lambda j, t: (score(0, j, s0, m0), t)[1], 0)
        for head in range(2 * PAIRS):
            s, m = bufs[head % 2]
            sn, mn = bufs[(head + 1) % 2]
            settle(m)
            acc[0:rows, :] = jnp.zeros((rows, 128), jnp.float32)
            more = head + 1 < 2 * PAIRS
            if more:
                begin(mn)

            def step(j, t, head=head, s=s, m=m, sn=sn, mn=mn, more=more):
                if more:
                    score(head + 1, j, sn, mn)
                weigh(head, j, s, m)
                return t

            lax.fori_loop(0, chunks, step, 0)
            finish(head)

    def frame_body(f, first):
        blocks = counts[f]
        for k in range(1, 2 * SIDE + 1):
            blocks += counts[f + k]
        own = counts[SIDE + f]
        for n in range(1, MOSTB + 1):

            @pl.when(own == n)
            def _(n=n):
                frame_rows(f, first, blocks, n * BLK)
                if n < MOSTB:
                    out[f, n * BLK :, :] = jnp.zeros((ROWS - n * BLK, GW), jnp.bfloat16)

        return first + counts[f]

    lax.fori_loop(0, SIDE, frame_body, 0)


def attend(counts, q, kv):
    vmem = pl.BlockSpec(memory_space=pltpu.VMEM)
    return pl.pallas_call(
        attend_kernel,
        out_shape=jax.ShapeDtypeStruct((SIDE, ROWS, GW), jnp.bfloat16),
        in_specs=[pl.BlockSpec(memory_space=pltpu.SMEM), vmem, vmem],
        out_specs=vmem,
        scratch_shapes=[
            pltpu.VMEM((PAIRS, KROWS, 128), jnp.bfloat16),
            pltpu.VMEM((PAIRS, 2, KROWS, 128), jnp.bfloat16),
            pltpu.VMEM((2 * PAIRS, ROWS, 128), jnp.bfloat16),
            pltpu.VMEM((NCH, ROWS, CH), jnp.float32),
            pltpu.VMEM((NCH, ROWS, CH), jnp.float32),
            pltpu.VMEM((ROWS, 128), jnp.float32),
            pltpu.VMEM((ROWS, 128), jnp.float32),
            pltpu.VMEM((ROWS, 128), jnp.float32),
        ],
        compiler_params=pltpu.CompilerParams(vmem_limit_bytes=VMEM),
        name="attend",
    )(counts, q, kv)


def project_kernel(part, w, out, got, wbuf, total, wsem, ss, rs):
    y, x = place()
    order = (0, 1, 3, 2)
    loads = []
    for i, delta in enumerate(order):
        row = pl.multiple_of(((x - delta) % SIDE) * GW, GW)
        load = pltpu.make_async_copy(w.at[pl.ds(row, GW), :], wbuf.at[i], wsem.at[i])
        load.start()
        loads.append(load)
    barrier = pltpu.get_barrier_semaphore()
    for delta in (1, 2, 3):
        pl.semaphore_signal(barrier, inc=1, device_id=device(y, x + delta), device_id_type=MESH)
    pl.semaphore_wait(barrier, 3)
    copies = {}
    for delta in (2, 1, 3):
        copies[delta] = pltpu.make_async_remote_copy(
            part.at[(x + delta) % SIDE], got.at[delta], ss.at[delta], rs.at[delta],
            device_id=device(y, x + delta), device_id_type=MESH,
        )
        copies[delta].start()
    for i, delta in enumerate(order):
        loads[i].wait()
        if delta:
            copies[delta].wait()

        def rows(r, carry, i=i, delta=delta):
            at = pl.ds(pl.multiple_of(r * BLK, BLK), BLK)
            block = got[delta, at, :] if delta else part[x, at, :]
            value = jnp.dot(block, wbuf[i], preferred_element_type=jnp.float32)
            if i:
                value += total[at, :]
            if i < SIDE - 1:
                total[at, :] = value
            else:
                scale = lax.rsqrt(jnp.mean(value * value, axis=-1, keepdims=True) + 1e-06)
                out[at, :] = (value * scale).astype(jnp.bfloat16)
            return carry

        lax.fori_loop(0, MOSTB, rows, 0)


def project(part, w_out):
    dma = pltpu.SemaphoreType.DMA
    vmem = pl.BlockSpec(memory_space=pltpu.VMEM)
    return pl.pallas_call(
        project_kernel,
        out_shape=jax.ShapeDtypeStruct((ROWS, D), jnp.bfloat16),
        in_specs=[vmem, pl.BlockSpec(memory_space=pl.ANY)],
        out_specs=vmem,
        scratch_shapes=[
            pltpu.VMEM((SIDE, ROWS, GW), jnp.bfloat16),
            pltpu.VMEM((SIDE, GW, D), jnp.bfloat16),
            pltpu.VMEM((ROWS, D), jnp.float32),
            dma((SIDE,)),
            dma((SIDE,)),
            dma((SIDE,)),
        ],
        compiler_params=pltpu.CompilerParams(
            collective_id=1, has_side_effects=True, vmem_limit_bytes=VMEM
        ),
        name="project",
    )(part, w_out)


def scatter_kernel(order, count, block, out):
    live = pl.program_id(0) < count[0]

    @pl.when(live)
    def _():
        out[...] = block[...]

    @pl.when(jnp.logical_not(live))
    def _():
        out[...] = jnp.zeros_like(out)


def scatter(order_row, count, normalized):
    blocks = order_row.shape[0]
    return pl.pallas_call(
        scatter_kernel,
        grid_spec=pltpu.PrefetchScalarGridSpec(
            num_scalar_prefetch=2,
            grid=(blocks,),
            in_specs=[pl.BlockSpec((BLK, D), lambda j, order, count: (jnp.minimum(j, MOSTB - 1), 0))],
            out_specs=pl.BlockSpec((BLK, D), lambda j, order, count: (order[j], 0)),
        ),
        out_shape=jax.ShapeDtypeStruct((blocks * BLK, D), jnp.bfloat16),
        name="scatter",
    )(order_row, count, normalized)


def shards(tokens, keep_count, keep_order, w_qkv, w_out):
    here = lax.axis_index("frame")
    order_row = keep_order[0]
    own_count = lax.dynamic_slice(keep_count, (here,), (1,))
    row = here // SIDE
    around = lax.dynamic_slice(
        jnp.concatenate([keep_count, keep_count]), (((row + SIDE - 1) % SIDE) * SIDE,), (3 * SIDE,)
    )
    normed = norm_kept(order_row, tokens)
    kv, q = exchange(normed, w_qkv)
    part = attend(around, q, kv)
    normalized = project(part, w_out)
    return scatter(order_row, own_count, normalized)


def solution(mesh):
    return jax.shard_map(
        shards,
        mesh=mesh,
        in_specs=(P(("orbit", "frame"), None), P("orbit"), P(("orbit", "frame"), None), P(), P()),
        out_specs=P(("orbit", "frame"), None),
        check_vma=False,
    )
```

time: 364 us -> 158 us (0.43); the launches traced: 358 us -> 157 us
  matrix products: 175 us -> 0 us
  Pallas kernels: 0 us -> 154 us
  other arithmetic: 86.6 us -> 0.8 us
  starting transfers between devices: 44.6 us -> 0 us
  local copies, waits for them, and re-layouts: 45.1 us -> 1.95 us
  between operations: 6.78 us -> 0.02 us
    dot_general x21 -> x0, matrix products: 175 us -> none  [the longest x9 89.1 us: frame_partial(): jnp.einsum('rhs,shd->rhd', weights.astype(jnp.bfloat16), v_heads, preferr...]
    pallas_call x0 -> x5, Pallas kernels: none -> 154 us  [the longest x1 68 us: exchange(): pl.pallas_call(exchange_kernel, out_shape=(jax.ShapeDtypeStruct((3 * SIDE...]
    reduce_sum x12 -> x0, other arithmetic: 82.7 us -> none  [the longest x9 71.9 us: frame_partial(): total = jnp.sum(weights, axis=-1)]
    ppermute x16 -> x0, starting transfers between devices: 44.6 us -> none  [shifted(): return lax.ppermute(value, axis, pairs)]
    ppermute x16 -> x0, local copies, waits for them, and re-layouts: 29.9 us -> none  [shifted(): return lax.ppermute(value, axis, pairs)]
    slice x4 -> x0, local copies, waits for them, and re-layouts: 7.18 us -> none  [the longest x2 3.38 us: shards(): query = qkv[:, :width]]
    reshape x2 -> x0, local copies, waits for them, and re-layouts: 5.99 us -> none  [the longest x1 3.93 us: shards(): return placed.astype(jnp.bfloat16).reshape(nblocks * BLK, D)]
  transfers between devices with their start and end apart: 16 -> 0, of which waited for: 0 -> 0; matrix products, arithmetic and copies ran while one was open for 72% -> 0% of each run, Pallas kernels for 0% -> 0%
where the time goes in v1:
time: 158 us; the launch traced here: 157 us
  Pallas kernels  154 us (97%)
  local copies, waits for them, and re-layouts  1.95 us (1%)
    pallas_call x1, Pallas kernels, exchange(): pl.pallas_call(exchange_kernel, out_shape=(jax.ShapeDtypeStruct((3 * SIDE...  68 us
    pallas_call x1, Pallas kernels, attend(): pl.pallas_call(attend_kernel, out_shape=jax.ShapeDtypeStruct((SIDE, ROWS,...  60.7 us
    pallas_call x1, Pallas kernels, project(): pl.pallas_call(project_kernel, out_shape=jax.ShapeDtypeStruct((ROWS, D),...  17.2 us
    pallas_call x1, Pallas kernels, scatter(): pl.pallas_call(scatter_kernel, grid_spec=pltpu.PrefetchScalarGridSpec(num...  4.61 us
    pallas_call x1, Pallas kernels, norm_kept(): pl.pallas_call(norm_kernel, grid_spec=pltpu.PrefetchScalarGridSpec(num_sc...  4.05 us

profile of v1, /device:TPU:64, one launch (start us, length us, event | category | flops | bytes accessed | tf_op | source)
XLA Modules:
  0.0 157.3 jit_solution(907746250226648664)
XLA Ops:
  0.0 1.3 dynamic_slice.6.count
  1.3 0.8 pad_add_fusion
  2.1 0.6 dynamic_slice.7.counts
  2.8 4.0 %norm_kept.1.normed = bf16[384,1536]{1,0:T(8,128)(2,1)} custom-call(s32[4]{0:T(128)} %bitcast.1, bf16[512,1536]{1,0:T(8,128)(2,1)} %tok.1), custom_call_target="tpu_custom_call" | custom-call | tf_op jit(solution)/shard_map/norm_kept/pallas_call | solution.py:43
  6.8 68.0 %exchange.1 = (bf16[12,384,768]{2,1,0:T(8,128)(2,1)}, bf16[4,384,384]{2,1,0:T(8,128)(2,1)}) custom-call(bf16[384,1536]{1,0:T(8,128)(2,1)} %norm_kept.1.normed, bf16[1536,4608]{1,0:T(8,128)(2,1)} %w.2), custom_call_target="tpu_custom_call" | custom-call | tf_op jit(solution)/shard_map/exchange/pallas_call | solution.py:146
  74.8 60.7 %attend.1.part = bf16[4,384,384]{2,1,0:T(8,128)(2,1)} custom-call(s32[12]{0:T(128)} %dynamic_slice.7.counts, bf16[4,384,384]{2,1,0:T(8,128)(2,1)} %get-tuple-element.7.q, bf16[12,384,768]{2,1,0:T(8,128)(2,1)} %get-tuple-element.8.kv), custom_call_target="tpu_custom_call" | custom-call | tf_op jit(solution)/shard_map/attend/pallas_call | solution.py:292
  135.5 17.2 %project.1.block = bf16[384,1536]{1,0:T(8,128)(2,1)} custom-call(bf16[4,384,384]{2,1,0:T(8,128)(2,1)} %attend.1.part, bf16[1536,1536]{1,0:T(8,128)(2,1)} %w.3), custom_call_target="tpu_custom_call" | custom-call | tf_op jit(solution)/shard_map/project/pallas_call | solution.py:356
  152.7 4.6 %scatter.1 = bf16[512,1536]{1,0:T(8,128)(2,1)} custom-call(s32[4]{0:T(128)} %bitcast.2, s32[1]{0:T(128)} %dynamic_slice.6.count, bf16[384,1536]{1,0:T(8,128)(2,1)} %project.1.block), custom_call_target="tpu_custom_call" | custom-call | tf_op jit(solution)/shard_map/scatter/pallas_call | solution.py:390

commit v2 on v1

v2 whole, which is shorter than its diff:
```python
import functools

import jax
import jax.numpy as jnp
from jax import lax
from jax.experimental import pallas as pl
from jax.experimental.pallas import tpu as pltpu
from jax.sharding import PartitionSpec as P

D = 1536
HEADS = 24
HEAD_DIM = 64
BLK = 128
MOSTB = 3
ROWS = MOSTB * BLK
SIDE = 4
GW = 384
PAIRS = 3
CH = 512
NCH = 7
KROWS = 36 * BLK + CH
SCALE = HEAD_DIM ** (-0.5) * 1.4426950408889634
VMEM = 60 * 2**20
MESH = pl.DeviceIdType.MESH


def place():
    me = lax.axis_index("frame")
    return me // SIDE, me % SIDE


def device(y, x):
    return {"frame": (y % SIDE) * SIDE + x % SIDE}


def norm_kernel(order, tok, out):
    wide = tok[...].astype(jnp.float32)
    scale = lax.rsqrt(jnp.mean(wide * wide, axis=-1, keepdims=True) + 1e-06)
    out[...] = (wide * scale).astype(jnp.bfloat16)


def norm_kept(order_row, tokens):
    return pl.pallas_call(
        norm_kernel,
        grid_spec=pltpu.PrefetchScalarGridSpec(
            num_scalar_prefetch=1,
            grid=(MOSTB,),
            in_specs=[pl.BlockSpec((BLK, D), lambda j, order: (order[0, j], 0))],
            out_specs=pl.BlockSpec((BLK, D), lambda j, order: (j, 0)),
        ),
        out_shape=jax.ShapeDtypeStruct((ROWS, D), jnp.bfloat16),
        name="norm_kept",
    )(order_row, tokens)


BLOCKS = ((0, 1), (0, 2), (1, 1), (1, 2), (3, 1), (3, 2), (2, 1), (2, 2), (1, 0), (3, 0), (2, 0), (0, 0))
FW = 256
LW = GW - FW


def exchange_kernel(
    normed, w, below, row, above, last, q, wbuf, kvs, lasts, qs,
    wsem, xs, xr, ls, lr, qss, qsr, ys, yr,
):
    y, x = place()
    loads = []
    for i, (delta, kind) in enumerate(BLOCKS):
        col = pl.multiple_of(kind * (HEADS * HEAD_DIM) + ((x + delta) % SIDE) * GW, 128)
        load = pltpu.make_async_copy(w.at[:, pl.ds(col, GW)], wbuf.at[i], wsem.at[i])
        load.start()
        loads.append(load)
    barrier = pltpu.get_barrier_semaphore()
    peers = [(0, 1), (0, 2), (0, 3), (1, 0), (3, 0)]
    for dy, dx in peers:
        pl.semaphore_signal(barrier, inc=1, device_id=device(y + dy, x + dx), device_id_type=MESH)
    pl.semaphore_wait(barrier, len(peers))

    def product(i, put):
        loads[i].wait()

        def rows(r, carry):
            at = pl.ds(pl.multiple_of(r * BLK, BLK), BLK)
            value = jnp.dot(normed[at, :], wbuf[i], preferred_element_type=jnp.float32)
            put(at, value)
            return carry

        lax.fori_loop(0, MOSTB, rows, 0)

    def across(src, dst, send, recv, delta):
        return pltpu.make_async_remote_copy(
            src.at[delta], dst.at[delta], send.at[delta], recv.at[delta],
            device_id=device(y, x + delta), device_id_type=MESH,
        )

    first = {delta: across(kvs, row, xs, xr, delta) for delta in (1, 2, 3)}
    later = {delta: across(lasts, last, ls, lr, delta) for delta in (1, 2, 3)}
    query = {delta: across(qs, q, qss, qsr, delta) for delta in (1, 2, 3)}
    sent = []

    def up_down(delta):
        for way, (dy, to) in enumerate(((1, below), (-1, above))):
            copy = pltpu.make_async_remote_copy(
                row.at[delta], to.at[delta], ys.at[way, delta], yr.at[way, delta],
                device_id=device(y + dy, x), device_id_type=MESH,
            )
            copy.start()
            sent.append(copy)

    for i, (delta, kind) in enumerate(BLOCKS):
        if kind == 0:
            to = q if delta == 0 else qs

            def put(at, value, delta=delta, to=to):
                to[delta, at, :] = (value * SCALE).astype(jnp.bfloat16)
        else:
            to, rest = (row, last) if delta == 0 else (kvs, lasts)

            def put(at, value, delta=delta, kind=kind, to=to, rest=rest):
                value = value.astype(jnp.bfloat16)
                to[delta, at, pl.ds((kind - 1) * FW, FW)] = value[:, :FW]
                rest[delta, at, pl.ds((kind - 1) * LW, LW)] = value[:, FW:]

        product(i, put)
        if kind == 2:
            if delta == 0:
                up_down(0)
            elif delta != 2:
                first[delta].start()
    first[1].wait()
    up_down(1)
    first[2].start()
    first[3].wait()
    up_down(3)
    for delta in (1, 3, 2):
        query[delta].start()
    first[2].wait()
    up_down(2)
    for delta in (1, 3, 2):
        later[delta].start()
    for copy in [*query.values(), *later.values(), *sent]:
        copy.wait()


def exchange(normed, w_qkv):
    dma = pltpu.SemaphoreType.DMA
    vmem = pl.BlockSpec(memory_space=pltpu.VMEM)
    shapes = [(SIDE, ROWS, 2 * FW)] * 3 + [(SIDE, ROWS, 2 * LW), (SIDE, ROWS, GW)]
    return pl.pallas_call(
        exchange_kernel,
        out_shape=[jax.ShapeDtypeStruct(shape, jnp.bfloat16) for shape in shapes],
        in_specs=[vmem, pl.BlockSpec(memory_space=pl.ANY)],
        out_specs=[vmem] * 5,
        scratch_shapes=[
            pltpu.VMEM((len(BLOCKS), D, GW), jnp.bfloat16),
            pltpu.VMEM((SIDE, ROWS, 2 * FW), jnp.bfloat16),
            pltpu.VMEM((SIDE, ROWS, 2 * LW), jnp.bfloat16),
            pltpu.VMEM((SIDE, ROWS, GW), jnp.bfloat16),
            dma((len(BLOCKS),)),
            *[dma((SIDE,))] * 6,
            dma((2, SIDE)),
            dma((2, SIDE)),
        ],
        compiler_params=pltpu.CompilerParams(
            collective_id=0, has_side_effects=True, vmem_limit_bytes=34 * 2**20
        ),
        name="exchange",
    )(normed, w_qkv)


def attend_kernel(start, pairs, keep, q, below, row, above, out, live, keys, vals, masked, s0, s1, m0, m1, acc):
    y, x = place()
    for k in range(3 * SIDE):
        live[k] = keep[((y + SIDE - 1) * SIDE + k) % (SIDE * SIDE)]
    low = lax.broadcasted_iota(jnp.int32, (1, 128), 1) < HEAD_DIM
    one = jnp.ones((BLK, 128), jnp.bfloat16)
    counts = live
    total = 0
    for k, kv in enumerate((below, row, above)):

        def pack(slot, at, k=k, kv=kv):
            frame, block = slot // MOSTB, slot % MOSTB
            back = (x + SIDE - frame) % SIDE
            used = block < counts[k * SIDE + frame]

            @pl.when(used)
            def _():
                rows = pl.ds(pl.multiple_of(block * BLK, BLK), BLK)
                to = pl.ds(pl.multiple_of(at * BLK, BLK), BLK)
                for c in range(pairs):
                    keys[c, to, :] = kv[back, rows, c * 128 : (c + 1) * 128]
                    v = kv[back, rows, (pairs + c) * 128 : (pairs + c + 1) * 128]
                    vals[c, 0, to, :] = jnp.where(low, v, one)
                    vals[c, 1, to, :] = jnp.where(low, one, v)

            return at + used.astype(jnp.int32)

        total = lax.fori_loop(0, SIDE * MOSTB, pack, total)
    tail = pl.ds(pl.multiple_of(total * BLK, BLK), CH)
    for c in range(pairs):
        keys[c, tail, :] = jnp.zeros((CH, 128), jnp.bfloat16)
        for h in range(2):
            vals[c, h, tail, :] = jnp.zeros((CH, 128), jnp.bfloat16)

    def frame_rows(d, first, blocks, rows):
        chunks = pl.cdiv(blocks, CH // BLK)
        limit = blocks * BLK
        for c in range(pairs):
            value = q[d, 0:rows, (start + c) * 128 : (start + c + 1) * 128]
            zero = jnp.zeros_like(value)
            masked[2 * c, 0:rows, :] = jnp.where(low, value, zero)
            masked[2 * c + 1, 0:rows, :] = jnp.where(low, zero, value)

        def score(head, j, s, m):
            at = pl.ds(pl.multiple_of(first * BLK + j * CH, BLK), CH)
            value = lax.dot_general(
                masked[head, 0:rows, :], keys[head // 2, at, :],
                (((1,), (1,)), ((), ())), preferred_element_type=jnp.float32,
            )
            col = lax.broadcasted_iota(jnp.int32, (1, CH), 1) + j * CH
            value = jnp.where(col < limit, value, -1e30)
            s[j, 0:rows, :] = value
            top = m[0:rows, :]
            for t in range(CH // 128):
                top = jnp.maximum(top, value[:, t * 128 : (t + 1) * 128])
            m[0:rows, :] = top

        def begin(m):
            m[0:rows, :] = jnp.full((rows, 128), -1e30, jnp.float32)

        def settle(m):
            m[0:rows, :] = jnp.broadcast_to(
                jnp.max(m[0:rows, :], axis=1, keepdims=True), (rows, 128)
            )

        def weigh(head, j, s, m):
            at = pl.ds(pl.multiple_of(first * BLK + j * CH, BLK), CH)
            top = m[0:rows, :]
            value = s[j, 0:rows, :]
            p = jnp.exp2(value - jnp.concatenate([top] * (CH // 128), axis=1)).astype(jnp.bfloat16)
            acc[0:rows, :] += jnp.dot(
                p, vals[head // 2, head % 2, at, :], preferred_element_type=jnp.float32
            )

        def finish(head):
            value = acc[0:rows, :]
            ratio = value / pltpu.roll(value, HEAD_DIM, 1)
            cols = slice((head // 2) * 128, (head // 2 + 1) * 128)
            if head % 2 == 0:
                out[d, 0:rows, cols] = ratio.astype(jnp.bfloat16)
            else:
                before = out[d, 0:rows, cols]
                out[d, 0:rows, cols] = jnp.where(low, before, ratio.astype(jnp.bfloat16))

        bufs = ((s0, m0), (s1, m1))
        begin(m0)
        lax.fori_loop(0, chunks, lambda j, t: (score(0, j, s0, m0), t)[1], 0)
        for head in range(2 * pairs):
            s, m = bufs[head % 2]
            sn, mn = bufs[(head + 1) % 2]
            settle(m)
            acc[0:rows, :] = jnp.zeros((rows, 128), jnp.float32)
            more = head + 1 < 2 * pairs
            if more:
                begin(mn)

            def step(j, t, head=head, s=s, m=m, sn=sn, mn=mn, more=more):
                if more:
                    score(head + 1, j, sn, mn)
                weigh(head, j, s, m)
                return t

            lax.fori_loop(0, chunks, step, 0)
            finish(head)

    def frame_body(f, first):
        blocks = counts[f]
        for k in range(1, 2 * SIDE + 1):
            blocks += counts[f + k]
        own = counts[SIDE + f]
        d = (x + SIDE - f) % SIDE
        for n in range(1, MOSTB + 1):

            @pl.when(own == n)
            def _(n=n):
                frame_rows(d, first, blocks, n * BLK)
                if n < MOSTB:
                    out[d, n * BLK :, :] = jnp.zeros((ROWS - n * BLK, pairs * 128), jnp.bfloat16)

        return first + counts[f]

    lax.fori_loop(0, SIDE, frame_body, 0)


def attend(start, pairs, keep_count, q, below, row, above):
    vmem = pl.BlockSpec(memory_space=pltpu.VMEM)
    return pl.pallas_call(
        functools.partial(attend_kernel, start, pairs),
        out_shape=jax.ShapeDtypeStruct((SIDE, ROWS, pairs * 128), jnp.bfloat16),
        in_specs=[pl.BlockSpec(memory_space=pltpu.SMEM)] + [vmem] * 4,
        out_specs=vmem,
        scratch_shapes=[
            pltpu.SMEM((3 * SIDE,), jnp.int32),
            pltpu.VMEM((pairs, KROWS, 128), jnp.bfloat16),
            pltpu.VMEM((pairs, 2, KROWS, 128), jnp.bfloat16),
            pltpu.VMEM((2 * pairs, ROWS, 128), jnp.bfloat16),
            pltpu.VMEM((NCH, ROWS, CH), jnp.float32),
            pltpu.VMEM((NCH, ROWS, CH), jnp.float32),
            pltpu.VMEM((ROWS, 128), jnp.float32),
            pltpu.VMEM((ROWS, 128), jnp.float32),
            pltpu.VMEM((ROWS, 128), jnp.float32),
        ],
        compiler_params=pltpu.CompilerParams(vmem_limit_bytes=VMEM // 2),
        cost_estimate=pl.CostEstimate(
            flops=pairs * 18 * 10**9, bytes_accessed=pairs * 2**21, transcendentals=0
        ),
        name="attend",
    )(keep_count, q, below, row, above)


def project_kernel(part, rest, w, out, got, wbuf, total, wsem, ss, rs, ts, tr):
    y, x = place()
    order = (0, 1, 3, 2)
    loads = []
    for i, delta in enumerate(order):
        row = pl.multiple_of(((x - delta) % SIDE) * GW, GW)
        load = pltpu.make_async_copy(w.at[pl.ds(row, GW), :], wbuf.at[i], wsem.at[i])
        load.start()
        loads.append(load)
    barrier = pltpu.get_barrier_semaphore()
    for delta in (1, 2, 3):
        pl.semaphore_signal(barrier, inc=1, device_id=device(y, x + delta), device_id_type=MESH)
    pl.semaphore_wait(barrier, 3)
    copies = {}
    for delta in (2, 1, 3):
        copies[delta] = [
            pltpu.make_async_remote_copy(
                src.at[(SIDE - delta) % SIDE], got.at[delta, :, cols], send.at[delta], recv.at[delta],
                device_id=device(y, x + delta), device_id_type=MESH,
            )
            for src, cols, send, recv in (
                (part, pl.ds(0, FW), ss, rs),
                (rest, pl.ds(FW, LW), ts, tr),
            )
        ]
        for copy in copies[delta]:
            copy.start()
    got[0, :, :FW] = part[0]
    got[0, :, FW:] = rest[0]
    for i, delta in enumerate(order):
        loads[i].wait()
        if delta:
            for copy in copies[delta]:
                copy.wait()

        def rows(r, carry, i=i, delta=delta):
            at = pl.ds(pl.multiple_of(r * BLK, BLK), BLK)
            value = jnp.dot(got[delta, at, :], wbuf[i], preferred_element_type=jnp.float32)
            if i:
                value += total[at, :]
            if i < SIDE - 1:
                total[at, :] = value
            else:
                scale = lax.rsqrt(jnp.mean(value * value, axis=-1, keepdims=True) + 1e-06)
                out[at, :] = (value * scale).astype(jnp.bfloat16)
            return carry

        lax.fori_loop(0, MOSTB, rows, 0)


def project(part, rest, w_out):
    dma = pltpu.SemaphoreType.DMA
    vmem = pl.BlockSpec(memory_space=pltpu.VMEM)
    return pl.pallas_call(
        project_kernel,
        out_shape=jax.ShapeDtypeStruct((ROWS, D), jnp.bfloat16),
        in_specs=[vmem, vmem, pl.BlockSpec(memory_space=pl.ANY)],
        out_specs=vmem,
        scratch_shapes=[
            pltpu.VMEM((SIDE, ROWS, GW), jnp.bfloat16),
            pltpu.VMEM((SIDE, GW, D), jnp.bfloat16),
            pltpu.VMEM((ROWS, D), jnp.float32),
            *[dma((SIDE,))] * 5,
        ],
        compiler_params=pltpu.CompilerParams(
            collective_id=1, has_side_effects=True, vmem_limit_bytes=24 * 2**20
        ),
        name="project",
    )(part, rest, w_out)


def scatter_kernel(order, count, block, out):
    live = pl.program_id(0) < count[lax.axis_index("frame")]

    @pl.when(live)
    def _():
        out[...] = block[...]

    @pl.when(jnp.logical_not(live))
    def _():
        out[...] = jnp.zeros_like(out)


def scatter(order_row, count, normalized):
    blocks = order_row.shape[1]
    return pl.pallas_call(
        scatter_kernel,
        grid_spec=pltpu.PrefetchScalarGridSpec(
            num_scalar_prefetch=2,
            grid=(blocks,),
            in_specs=[pl.BlockSpec((BLK, D), lambda j, order, count: (jnp.minimum(j, MOSTB - 1), 0))],
            out_specs=pl.BlockSpec((BLK, D), lambda j, order, count: (order[0, j], 0)),
        ),
        out_shape=jax.ShapeDtypeStruct((blocks * BLK, D), jnp.bfloat16),
        name="scatter",
    )(order_row, count, normalized)


def shifted(value, steps):
    count = SIDE * SIDE
    return lax.ppermute(value, "frame", [(f, (f + steps) % count) for f in range(count)])


def shards(tokens, keep_count, keep_order, w_qkv, w_out):
    normed = norm_kept(keep_order, tokens)
    below, row, above, last, q = exchange(normed, w_qkv)
    last_below = shifted(last, SIDE)
    last_above = shifted(last, -SIDE)
    part = attend(0, 2, keep_count, q, below, row, above)
    rest = attend(2, 1, keep_count, q, last_below, last, last_above)
    normalized = project(part, rest, w_out)
    return scatter(keep_order, keep_count, normalized)


def solution(mesh):
    return jax.shard_map(
        shards,
        mesh=mesh,
        in_specs=(P(("orbit", "frame"), None), P("orbit"), P(("orbit", "frame"), None), P(), P()),
        out_specs=P(("orbit", "frame"), None),
        check_vma=False,
    )
```

time: 158 us -> 145 us (0.918)
  the two profiles are of different devices: /device:TPU:64 before, /device:TPU:82 now
where the time goes in v2:
time: 145 us; the launch traced here: 144 us
  Pallas kernels  140 us (97%)
  local copies, waits for them, and re-layouts  2.3 us (2%)
  starting transfers between devices  2.1 us (1%)
    pallas_call x2, Pallas kernels, attend(): pl.pallas_call(functools.partial(attend_kernel, start, pairs), out_shape=...  62.4 us
    pallas_call x1, Pallas kernels, exchange(): pl.pallas_call(exchange_kernel, out_shape=[jax.ShapeDtypeStruct(shape, jn...  49.3 us
    pallas_call x1, Pallas kernels, project(): pl.pallas_call(project_kernel, out_shape=jax.ShapeDtypeStruct((ROWS, D),...  20.2 us
    pallas_call x1, Pallas kernels, norm_kept(): pl.pallas_call(norm_kernel, grid_spec=pltpu.PrefetchScalarGridSpec(num_sc...  4.05 us
    pallas_call x1, Pallas kernels, scatter(): pl.pallas_call(scatter_kernel, grid_spec=pltpu.PrefetchScalarGridSpec(num...  3.93 us
  transfers between devices with their start and end apart: 2, of which 0 were waited for; matrix products, arithmetic and copies ran while one was open for 0% of the time, Pallas kernels for 28%

profile of v2, /device:TPU:82, one launch (start us, length us, event | category | flops | bytes accessed | tf_op | source)
XLA Modules:
  0.0 144.3 jit_solution(9263612860515155507)
XLA Ops:
  0.0 4.0 %norm_kept.1.normed = bf16[384,1536]{1,0:T(8,128)(2,1)} custom-call(s32[1,4]{1,0:T(1,128)} %order.3, bf16[512,1536]{1,0:T(8,128)(2,1)} %tok.1), custom_call_target="tpu_custom_call" | custom-call | tf_op jit(solution)/shard_map/norm_kept/pallas_call | solution.py:43
  4.1 0.0 copy-start.1
  4.1 1.3 copy-done.1
  5.3 0.0 copy-start.2
  5.3 0.0 slice-start
  5.3 49.3 %exchange.1 = (bf16[4,384,512]{2,1,0:T(8,128)(2,1)S(1)}, bf16[4,384,512]{2,1,0:T(8,128)(2,1)S(1)}, bf16[4,384,512]{2,1,0:T(8,128)(2,1)S(1)}, bf16[4,384,256]{2,1,0:T(8,128)(2,1)S(1)}, bf16[4,384,384]{2,1,0:T(8,128)(2,1)S(1)}) custom-call(bf16[384,1536]{1,0:T(8,128)(2,1)S(1)} %copy-done.1, bf16[1536,4608]{1,0:T(8,128)(2,1)} %w.2), custom_call_target="tpu_custom_call" | custom-call | tf_op jit(solution)/shard_map/exchange/pallas_call | solution.py:148
  54.6 0.5 collective-permute-start.1
  55.1 1.6 %collective-permute-start = (bf16[4,384,256]{2,1,0:T(8,128)(2,1)S(1)}, bf16[4,384,256]{2,1,0:T(8,128)(2,1)S(1)}, u32[]{:S(2)}, u32[]{:S(2)}) collective-permute-start(bf16[4,384,256]{2,1,0:T(8,128)(2,1)S(1)} %get-tuple-element.14.row), channel_id=1, source_target_pairs={{0,32},{8,40},{16,48},{24,56},{32,64},{40,72},{48,80},{56,88},{64,... | collective-permute-start | bytes 2359304 | tf_op jit(solution)/shard_map/ppermute | solution.py:420
  56.7 0.0 copy-done.2
  56.7 0.0 slice-start.1
  56.7 39.8 %attend.2.part = bf16[4,384,256]{2,1,0:T(8,128)(2,1)S(1)} custom-call(s32[16]{0:T(128)S(1)} %copy-done.2, bf16[4,384,384]{2,1,0:T(8,128)(2,1)S(1)} %get-tuple-element.10.q, bf16[4,384,512]{2,1,0:T(8,128)(2,1)S(1)} %get-tuple-element.11.below, bf16[4,384,512]{2,1,0:T(8,128)(2,1)S(1)} %get-tuple-element.12.row, bf16[4,384,512]{2,1,0:T(8,128)(2,1)S(1)} %get-tuple-element.13.above), custom_call_target="tpu_custom_call" | custom-call | flops 35999997952 | bytes 4194304 | tf_op jit(solution)/shard_map/attend/pallas_call | solution.py:296
  96.5 0.0 collective-permute-done.1.above
  96.5 0.0 collective-permute-done.below
  96.5 22.6 %attend.3.rest = bf16[4,384,128]{2,1,0:T(8,128)(2,1)S(1)} custom-call(s32[16]{0:T(128)S(1)} %copy-done.2, bf16[4,384,384]{2,1,0:T(8,128)(2,1)S(1)} %get-tuple-element.10.q, bf16[4,384,256]{2,1,0:T(8,128)(2,1)S(1)} %collective-permute-done.below, bf16[4,384,256]{2,1,0:T(8,128)(2,1)S(1)} %get-tuple-element.14.row, ...), custom_call_target="tpu_custom_call" | custom-call | flops 17999998976 | bytes 2097152 | tf_op jit(solution)/shard_map/attend/pallas_call | solution.py:296
  119.1 0.0 slice-done
  119.1 0.0 slice-done.1
  119.1 20.2 %project.1.block = bf16[384,1536]{1,0:T(8,128)(2,1)S(1)} custom-call(bf16[4,384,256]{2,1,0:T(8,128)(2,1)S(1)} %attend.2.part, bf16[4,384,128]{2,1,0:T(8,128)(2,1)S(1)} %attend.3.rest, bf16[1536,1536]{1,0:T(8,128)(2,1)S(1)} %bitcast.1), custom_call_target="tpu_custom_call" | custom-call | tf_op jit(solution)/shard_map/project/pallas_call | solution.py:373
  139.4 0.0 copy-start
  139.4 1.0 copy-done
  140.4 3.9 %scatter.1 = bf16[512,1536]{1,0:T(8,128)(2,1)} custom-call(s32[1,4]{1,0:T(1,128)} %order.3, s32[16]{0:T(128)} %count.1, bf16[384,1536]{1,0:T(8,128)(2,1)} %copy-done), custom_call_target="tpu_custom_call" | custom-call | tf_op jit(solution)/shard_map/scatter/pallas_call | solution.py:405
  (1 shorter events, 0.0 us)
Async XLA Ops:
  4.1 1.3 copy-start.1
  5.3 51.4 %copy-start.2 = (s32[16]{0:T(128)S(1)}, s32[16]{0:T(128)}, u32[]{:S(2)}) copy-start(s32[16]{0:T(128)} %count.1) | copy-start | bytes 196
  5.3 113.8 %slice-start = ((s8[4718592]{0:T(1024)(128)(4,1)}), s8[524288]{0:T(1024)(128)(4,1)S(1)}, s32[]{:S(2)}) async-start(s8[4718592]{0:T(1024)(128)(4,1)} %bitcast), calls=%async_computation | async-start | bytes 1048576
  54.6 41.9 %collective-permute-start.1 = (bf16[4,384,256]{2,1,0:T(8,128)(2,1)S(1)}, bf16[4,384,256]{2,1,0:T(8,128)(2,1)S(1)}, u32[]{:S(2)}, u32[]{:S(2)}) collective-permute-start(bf16[4,384,256]{2,1,0:T(8,128)(2,1)S(1)} %get-tuple-element.14.row), channel_id=1, source_target_pairs={{0,96},{8,104},{16,112},{24,120},{32,0},{40,8},{48,16},{56,24},{64... | collective-permute-start | bytes 2359304 | tf_op jit(solution)/shard_map/ppermute | solution.py:420
  55.1 41.4 %collective-permute-start = (bf16[4,384,256]{2,1,0:T(8,128)(2,1)S(1)}, bf16[4,384,256]{2,1,0:T(8,128)(2,1)S(1)}, u32[]{:S(2)}, u32[]{:S(2)}) collective-permute-start(bf16[4,384,256]{2,1,0:T(8,128)(2,1)S(1)} %get-tuple-element.14.row), channel_id=1, source_target_pairs={{0,32},{8,40},{16,48},{24,56},{32,64},{40,72},{48,80},{56,88},{64,... | collective-permute-start | bytes 2359304 | tf_op jit(solution)/shard_map/ppermute | solution.py:420
  56.7 62.4 %slice-start.1 = ((s8[4718592]{0:T(1024)(128)(4,1)}), s8[4194304]{0:T(1024)(128)(4,1)S(1)}, s32[]{:S(2)}) async-start(s8[4718592]{0:T(1024)(128)(4,1)} %bitcast), calls=%async_computation.1 | async-start | bytes 8388608
  139.4 1.0 copy-start

commit v3 on v2

--- a/solution.py
+++ b/solution.py
@@ -15,12 +15,10 @@
 ROWS = MOSTB * BLK
 SIDE = 4
 GW = 384
-PAIRS = 3
-CH = 512
-NCH = 7
+CH = 1024
+WINDOW = 28 * BLK
 KROWS = 36 * BLK + CH
 SCALE = HEAD_DIM ** (-0.5) * 1.4426950408889634
-VMEM = 60 * 2**20
 MESH = pl.DeviceIdType.MESH
 
 
@@ -202,75 +200,75 @@
             vals[c, h, tail, :] = jnp.zeros((CH, 128), jnp.bfloat16)
 
     def frame_rows(d, first, blocks, rows):
-        chunks = pl.cdiv(blocks, CH // BLK)
-        limit = blocks * BLK
+        full, left = blocks // (CH // BLK), blocks % (CH // BLK)
         for c in range(pairs):
             value = q[d, 0:rows, (start + c) * 128 : (start + c + 1) * 128]
             zero = jnp.zeros_like(value)
             masked[2 * c, 0:rows, :] = jnp.where(low, value, zero)
             masked[2 * c + 1, 0:rows, :] = jnp.where(low, zero, value)
 
-        def score(head, j, s, m):
-            at = pl.ds(pl.multiple_of(first * BLK + j * CH, BLK), CH)
-            value = lax.dot_general(
-                masked[head, 0:rows, :], keys[head // 2, at, :],
-                (((1,), (1,)), ((), ())), preferred_element_type=jnp.float32,
+        def span(j, width):
+            return (
+                pl.ds(pl.multiple_of(first * BLK + j * CH, BLK), width),
+                pl.ds(pl.multiple_of(j * CH, BLK), width),
             )
-            col = lax.broadcasted_iota(jnp.int32, (1, CH), 1) + j * CH
-            value = jnp.where(col < limit, value, -1e30)
-            s[j, 0:rows, :] = value
-            top = m[0:rows, :]
-            for t in range(CH // 128):
-                top = jnp.maximum(top, value[:, t * 128 : (t + 1) * 128])
-            m[0:rows, :] = top
-
-        def begin(m):
-            m[0:rows, :] = jnp.full((rows, 128), -1e30, jnp.float32)
-
-        def settle(m):
-            m[0:rows, :] = jnp.broadcast_to(
-                jnp.max(m[0:rows, :], axis=1, keepdims=True), (rows, 128)
-            )
-
-        def weigh(head, j, s, m):
-            at = pl.ds(pl.multiple_of(first * BLK + j * CH, BLK), CH)
-            top = m[0:rows, :]
-            value = s[j, 0:rows, :]
-            p = jnp.exp2(value - jnp.concatenate([top] * (CH // 128), axis=1)).astype(jnp.bfloat16)
-            acc[0:rows, :] += jnp.dot(
-                p, vals[head // 2, head % 2, at, :], preferred_element_type=jnp.float32
-            )
-
-        def finish(head):
-            value = acc[0:rows, :]
-            ratio = value / pltpu.roll(value, HEAD_DIM, 1)
-            cols = slice((head // 2) * 128, (head // 2 + 1) * 128)
-            if head % 2 == 0:
-                out[d, 0:rows, cols] = ratio.astype(jnp.bfloat16)
-            else:
-                before = out[d, 0:rows, cols]
-                out[d, 0:rows, cols] = jnp.where(low, before, ratio.astype(jnp.bfloat16))
+
+        def score(c, j, width, partial, s, m):
+            at, cols = span(j, width)
+            for h in range(2):
+                value = lax.dot_general(
+                    masked[2 * c + h, 0:rows, :], keys[c, at, :],
+                    (((1,), (1,)), ((), ())), preferred_element_type=jnp.float32,
+                )
+                if partial:
+                    col = lax.broadcasted_iota(jnp.int32, (1, width), 1)
+                    value = jnp.where(col < left * BLK, value, -1e30)
+                s[h, 0:rows, cols] = value
+                top = m[h, 0:rows, :]
+                for t in range(width // 128):
+                    top = jnp.maximum(top, value[:, t * 128 : (t + 1) * 128])
+                m[h, 0:rows, :] = top
+
+        def weigh(c, j, width, s, m):
+            at, cols = span(j, width)
+            for h in range(2):
+                top = jnp.concatenate([m[h, 0:rows, :]] * (width // 128), axis=1)
+                p = jnp.exp2(s[h, 0:rows, cols] - top).astype(jnp.bfloat16)
+                acc[h, 0:rows, :] += jnp.dot(p, vals[c, h, at, :], preferred_element_type=jnp.float32)
 
         bufs = ((s0, m0), (s1, m1))
-        begin(m0)
-        lax.fori_loop(0, chunks, lambda j, t: (score(0, j, s0, m0), t)[1], 0)
-        for head in range(2 * pairs):
-            s, m = bufs[head % 2]
-            sn, mn = bufs[(head + 1) % 2]
-            settle(m)
-            acc[0:rows, :] = jnp.zeros((rows, 128), jnp.float32)
-            more = head + 1 < 2 * pairs
-            if more:
-                begin(mn)
-
-            def step(j, t, head=head, s=s, m=m, sn=sn, mn=mn, more=more):
-                if more:
-                    score(head + 1, j, sn, mn)
-                weigh(head, j, s, m)
-                return t
-
-            lax.fori_loop(0, chunks, step, 0)
-            finish(head)
+        for stage in range(pairs + 1):
+            s, m = bufs[(stage + 1) % 2]
+            sn, mn = bufs[stage % 2]
+            if stage:
+                m[:, 0:rows, :] = jnp.broadcast_to(
+                    jnp.max(m[:, 0:rows, :], axis=2, keepdims=True), (2, rows, 128)
+                )
+                acc[:, 0:rows, :] = jnp.zeros((2, rows, 128), jnp.float32)
+            if stage < pairs:
+                mn[:, 0:rows, :] = jnp.full((2, rows, 128), -1e30, jnp.float32)
+
+            def step(j, width, partial, stage=stage, s=s, m=m, sn=sn, mn=mn):
+                if stage < pairs:
+                    score(stage, j, width, partial, sn, mn)
+                if stage:
+                    weigh(stage - 1, j, width, s, m)
+
+            lax.fori_loop(0, full, lambda j, t, step=step: (step(j, CH, False), t)[1], 0)
+
+            @pl.when((left > 0) & (left <= CH // BLK // 2))
+            def _(step=step):
+                step(full, CH // 2, True)
+
+            @pl.when(left > CH // BLK // 2)
+            def _(step=step):
+                step(full, CH, True)
+
+            if stage:
+                even, odd = acc[0, 0:rows, :], acc[1, 0:rows, :]
+                even = even / pltpu.roll(even, HEAD_DIM, 1)
+                odd = odd / pltpu.roll(odd, HEAD_DIM, 1)
+                out[d, 0:rows, (stage - 1) * 128 : stage * 128] = jnp.where(low, even, odd).astype(jnp.bfloat16)
 
     def frame_body(f, first):
         blocks = counts[f]
@@ -303,13 +301,11 @@
             pltpu.VMEM((pairs, KROWS, 128), jnp.bfloat16),
             pltpu.VMEM((pairs, 2, KROWS, 128), jnp.bfloat16),
             pltpu.VMEM((2 * pairs, ROWS, 128), jnp.bfloat16),
-            pltpu.VMEM((NCH, ROWS, CH), jnp.float32),
-            pltpu.VMEM((NCH, ROWS, CH), jnp.float32),
-            pltpu.VMEM((ROWS, 128), jnp.float32),
-            pltpu.VMEM((ROWS, 128), jnp.float32),
-            pltpu.VMEM((ROWS, 128), jnp.float32),
+            pltpu.VMEM((2, ROWS, WINDOW), jnp.float32),
+            pltpu.VMEM((2, ROWS, WINDOW), jnp.float32),
+            *[pltpu.VMEM((2, ROWS, 128), jnp.float32)] * 3,
         ],
-        compiler_params=pltpu.CompilerParams(vmem_limit_bytes=VMEM // 2),
+        compiler_params=pltpu.CompilerParams(vmem_limit_bytes=42 * 2**20),
         cost_estimate=pl.CostEstimate(
             flops=pairs * 18 * 10**9, bytes_accessed=pairs * 2**21, transcendentals=0
         ),

time: 145 us -> 126 us (0.87)
  the two profiles are of different devices: /device:TPU:82 before, /device:TPU:120 now
where the time goes in v3:
time: 126 us
  Pallas kernels  120 us (95%)
  starting transfers between devices  3.3 us (3%)
  local copies, waits for them, and re-layouts  2.3 us (2%)
    pallas_call x1, Pallas kernels, exchange(): pl.pallas_call(exchange_kernel, out_shape=[jax.ShapeDtypeStruct(shape, jn...  48.9 us
    pallas_call x2, Pallas kernels, attend(): pl.pallas_call(functools.partial(attend_kernel, start, pairs), out_shape=...  45.7 us
    pallas_call x1, Pallas kernels, project(): pl.pallas_call(project_kernel, out_shape=jax.ShapeDtypeStruct((ROWS, D),...  17.3 us
    pallas_call x1, Pallas kernels, norm_kept(): pl.pallas_call(norm_kernel, grid_spec=pltpu.PrefetchScalarGridSpec(num_sc...  4.05 us
    pallas_call x1, Pallas kernels, scatter(): pl.pallas_call(scatter_kernel, grid_spec=pltpu.PrefetchScalarGridSpec(num...  3.93 us
    ppermute x2, starting transfers between devices, shifted(): lax.ppermute(value, 'frame', [(f, (f + steps) % count) for f in range(cou...  3.3 us
  transfers between devices with their start and end apart: 2, of which 0 were waited for; matrix products, arithmetic and copies ran while one was open for 0% of the time, Pallas kernels for 23%

profile of v3, /device:TPU:120, one launch (start us, length us, event | category | flops | bytes accessed | tf_op | source)
XLA Modules:
  0.0 125.6 jit_solution(10215215125157840832)
XLA Ops:
  0.0 4.0 %norm_kept.1.normed = bf16[384,1536]{1,0:T(8,128)(2,1)} custom-call(s32[1,4]{1,0:T(1,128)} %order.3, bf16[512,1536]{1,0:T(8,128)(2,1)} %tok.1), custom_call_target="tpu_custom_call" | custom-call | tf_op jit(solution)/shard_map/norm_kept/pallas_call | solution.py:41
  4.1 0.0 copy-start.1
  4.1 1.3 %copy-done.1 = bf16[384,1536]{1,0:T(8,128)(2,1)S(1)} copy-done((bf16[384,1536]{1,0:T(8,128)(2,1)S(1)}, bf16[384,1536]{1,0:T(8,128)(2,1)}, u32[]{:S(2)}) %copy-start.1) | copy-done | bytes 1179672
  5.3 0.0 copy-start.2
  5.3 0.0 slice-start
  5.3 48.9 %exchange.1 = (bf16[4,384,512]{2,1,0:T(8,128)(2,1)S(1)}, bf16[4,384,512]{2,1,0:T(8,128)(2,1)S(1)}, bf16[4,384,512]{2,1,0:T(8,128)(2,1)S(1)}, bf16[4,384,256]{2,1,0:T(8,128)(2,1)S(1)}, bf16[4,384,384]{2,1,0:T(8,128)(2,1)S(1)}) custom-call(bf16[384,1536]{1,0:T(8,128)(2,1)S(1)} %copy-done.1, bf16[1536,4608]{1,0:T(8,128)(2,1)} %w.2), custom_call_target="tpu_custom_call" | custom-call | tf_op jit(solution)/shard_map/exchange/pallas_call | solution.py:146
  54.2 0.8 collective-permute-start.1
  55.0 2.5 %collective-permute-start = (bf16[4,384,256]{2,1,0:T(8,128)(2,1)S(1)}, bf16[4,384,256]{2,1,0:T(8,128)(2,1)S(1)}, u32[]{:S(2)}, u32[]{:S(2)}) collective-permute-start(bf16[4,384,256]{2,1,0:T(8,128)(2,1)S(1)} %get-tuple-element.14.row), channel_id=1, source_target_pairs={{0,32},{8,40},{16,48},{24,56},{32,64},{40,72},{48,80},{56,88},{64,... | collective-permute-start | bytes 2359304 | tf_op jit(solution)/shard_map/ppermute | solution.py:416
  57.5 0.0 copy-done.2
  57.5 0.0 slice-start.1
  57.5 29.3 %attend.2.part = bf16[4,384,256]{2,1,0:T(8,128)(2,1)S(1)} custom-call(s32[16]{0:T(128)S(1)} %copy-done.2, bf16[4,384,384]{2,1,0:T(8,128)(2,1)S(1)} %get-tuple-element.10.q, bf16[4,384,512]{2,1,0:T(8,128)(2,1)S(1)} %get-tuple-element.11.below, bf16[4,384,512]{2,1,0:T(8,128)(2,1)S(1)} %get-tuple-element.12.row, bf16[4,384,512]{2,1,0:T(8,128)(2,1)S(1)} %get-tuple-element.13.above), custom_call_target="tpu_custom_call" | custom-call | flops 35999997952 | bytes 4194304 | tf_op jit(solution)/shard_map/attend/pallas_call | solution.py:294
  86.8 0.0 collective-permute-done.1.above
  86.8 0.0 collective-permute-done.below
  86.8 16.4 %attend.3.rest = bf16[4,384,128]{2,1,0:T(8,128)(2,1)S(1)} custom-call(s32[16]{0:T(128)S(1)} %copy-done.2, bf16[4,384,384]{2,1,0:T(8,128)(2,1)S(1)} %get-tuple-element.10.q, bf16[4,384,256]{2,1,0:T(8,128)(2,1)S(1)} %collective-permute-done.below, bf16[4,384,256]{2,1,0:T(8,128)(2,1)S(1)} %get-tuple-element.14.row, ...), custom_call_target="tpu_custom_call" | custom-call | flops 17999998976 | bytes 2097152 | tf_op jit(solution)/shard_map/attend/pallas_call | solution.py:294
  103.3 0.0 slice-done
  103.3 0.0 slice-done.1
  103.3 17.3 %project.1.block = bf16[384,1536]{1,0:T(8,128)(2,1)S(1)} custom-call(bf16[4,384,256]{2,1,0:T(8,128)(2,1)S(1)} %attend.2.part, bf16[4,384,128]{2,1,0:T(8,128)(2,1)S(1)} %attend.3.rest, bf16[1536,1536]{1,0:T(8,128)(2,1)S(1)} %bitcast.1), custom_call_target="tpu_custom_call" | custom-call | tf_op jit(solution)/shard_map/project/pallas_call | solution.py:369
  120.6 0.0 copy-start
  120.6 1.0 copy-done
  121.6 3.9 %scatter.1 = bf16[512,1536]{1,0:T(8,128)(2,1)} custom-call(s32[1,4]{1,0:T(1,128)} %order.3, s32[16]{0:T(128)} %count.1, bf16[384,1536]{1,0:T(8,128)(2,1)} %copy-done), custom_call_target="tpu_custom_call" | custom-call | tf_op jit(solution)/shard_map/scatter/pallas_call | solution.py:401
  (1 shorter events, 0.0 us)
Async XLA Ops:
  4.1 1.3 %copy-start.1 = (bf16[384,1536]{1,0:T(8,128)(2,1)S(1)}, bf16[384,1536]{1,0:T(8,128)(2,1)}, u32[]{:S(2)}) copy-start(bf16[384,1536]{1,0:T(8,128)(2,1)} %norm_kept.1.normed) | copy-start | bytes 3538948
  5.3 52.2 %copy-start.2 = (s32[16]{0:T(128)S(1)}, s32[16]{0:T(128)}, u32[]{:S(2)}) copy-start(s32[16]{0:T(128)} %count.1) | copy-start | bytes 196
  5.3 97.9 %slice-start = ((s8[4718592]{0:T(1024)(128)(4,1)}), s8[4194304]{0:T(1024)(128)(4,1)S(1)}, s32[]{:S(2)}) async-start(s8[4718592]{0:T(1024)(128)(4,1)} %bitcast), calls=%async_computation | async-start | bytes 8388608
  54.2 32.6 %collective-permute-start.1 = (bf16[4,384,256]{2,1,0:T(8,128)(2,1)S(1)}, bf16[4,384,256]{2,1,0:T(8,128)(2,1)S(1)}, u32[]{:S(2)}, u32[]{:S(2)}) collective-permute-start(bf16[4,384,256]{2,1,0:T(8,128)(2,1)S(1)} %get-tuple-element.14.row), channel_id=1, source_target_pairs={{0,96},{8,104},{16,112},{24,120},{32,0},{40,8},{48,16},{56,24},{64... | collective-permute-start | bytes 2359304 | tf_op jit(solution)/shard_map/ppermute | solution.py:416
  55.0 31.8 %collective-permute-start = (bf16[4,384,256]{2,1,0:T(8,128)(2,1)S(1)}, bf16[4,384,256]{2,1,0:T(8,128)(2,1)S(1)}, u32[]{:S(2)}, u32[]{:S(2)}) collective-permute-start(bf16[4,384,256]{2,1,0:T(8,128)(2,1)S(1)} %get-tuple-element.14.row), channel_id=1, source_target_pairs={{0,32},{8,40},{16,48},{24,56},{32,64},{40,72},{48,80},{56,88},{64,... | collective-permute-start | bytes 2359304 | tf_op jit(solution)/shard_map/ppermute | solution.py:416
  57.5 45.8 %slice-start.1 = ((s8[4718592]{0:T(1024)(128)(4,1)}), s8[524288]{0:T(1024)(128)(4,1)S(1)}, s32[]{:S(2)}) async-start(s8[4718592]{0:T(1024)(128)(4,1)} %bitcast), calls=%async_computation.1 | async-start | bytes 1048576
  120.6 1.0 copy-start

commit v4 on v3

--- a/solution.py
+++ b/solution.py
@@ -31,27 +31,32 @@
     return {"frame": (y % SIDE) * SIDE + x % SIDE}
 
 
-def norm_kernel(order, tok, out):
-    wide = tok[...].astype(jnp.float32)
-    scale = lax.rsqrt(jnp.mean(wide * wide, axis=-1, keepdims=True) + 1e-06)
-    out[...] = (wide * scale).astype(jnp.bfloat16)
-
-
-def norm_kept(order_row, tokens):
+def norm_kernel(order, tokens, out, kept, sems):
+    loads = []
+    for j in range(MOSTB):
+        rows = pl.ds(pl.multiple_of(order[0, j] * BLK, BLK), BLK)
+        loads.append(pltpu.make_async_copy(tokens.at[rows, :], kept.at[j], sems.at[j]))
+        loads[j].start()
+    for j in range(MOSTB):
+        loads[j].wait()
+        wide = kept[j].astype(jnp.float32)
+        scale = lax.rsqrt(jnp.mean(wide * wide, axis=-1, keepdims=True) + 1e-06)
+        out[j * BLK : (j + 1) * BLK, :] = (wide * scale).astype(jnp.bfloat16)
+
+
+def norm_kept(keep_order, tokens):
     return pl.pallas_call(
         norm_kernel,
-        grid_spec=pltpu.PrefetchScalarGridSpec(
-            num_scalar_prefetch=1,
-            grid=(MOSTB,),
-            in_specs=[pl.BlockSpec((BLK, D), lambda j, order: (order[0, j], 0))],
-            out_specs=pl.BlockSpec((BLK, D), lambda j, order: (j, 0)),
-        ),
+        in_specs=[pl.BlockSpec(memory_space=pltpu.SMEM), pl.BlockSpec(memory_space=pltpu.HBM)],
+        out_specs=pl.BlockSpec(memory_space=pltpu.VMEM),
         out_shape=jax.ShapeDtypeStruct((ROWS, D), jnp.bfloat16),
+        scratch_shapes=[pltpu.VMEM((MOSTB, BLK, D), jnp.bfloat16), pltpu.SemaphoreType.DMA((MOSTB,))],
+        compiler_params=pltpu.CompilerParams(vmem_limit_bytes=12 * 2**20),
         name="norm_kept",
-    )(order_row, tokens)
-
-
-BLOCKS = ((0, 1), (0, 2), (1, 1), (1, 2), (3, 1), (3, 2), (2, 1), (2, 2), (1, 0), (3, 0), (2, 0), (0, 0))
+    )(keep_order, tokens)
+
+
+BLOCKS = ((1, 1), (1, 2), (0, 1), (0, 2), (3, 1), (3, 2), (2, 1), (2, 2), (1, 0), (3, 0), (2, 0), (0, 0))
 FW = 256
 LW = GW - FW
 
@@ -146,7 +151,7 @@
     return pl.pallas_call(
         exchange_kernel,
         out_shape=[jax.ShapeDtypeStruct(shape, jnp.bfloat16) for shape in shapes],
-        in_specs=[vmem, pl.BlockSpec(memory_space=pl.ANY)],
+        in_specs=[vmem, pl.BlockSpec(memory_space=pltpu.HBM)],
         out_specs=[vmem] * 5,
         scratch_shapes=[
             pltpu.VMEM((len(BLOCKS), D, GW), jnp.bfloat16),
@@ -313,7 +318,7 @@
     )(keep_count, q, below, row, above)
 
 
-def project_kernel(part, rest, w, out, got, wbuf, total, wsem, ss, rs, ts, tr):
+def project_kernel(own, one, two, three, rest, w, out, got, wbuf, total, wsem, ss, rs):
     y, x = place()
     order = (0, 1, 3, 2)
     loads = []
@@ -328,31 +333,35 @@
     pl.semaphore_wait(barrier, 3)
     copies = {}
     for delta in (2, 1, 3):
-        copies[delta] = [
-            pltpu.make_async_remote_copy(
-                src.at[(SIDE - delta) % SIDE], got.at[delta, :, cols], send.at[delta], recv.at[delta],
-                device_id=device(y, x + delta), device_id_type=MESH,
-            )
-            for src, cols, send, recv in (
-                (part, pl.ds(0, FW), ss, rs),
-                (rest, pl.ds(FW, LW), ts, tr),
-            )
-        ]
-        for copy in copies[delta]:
-            copy.start()
-    got[0, :, :FW] = part[0]
-    got[0, :, FW:] = rest[0]
+        copies[delta] = pltpu.make_async_remote_copy(
+            rest.at[(SIDE - delta) % SIDE], got.at[delta], ss.at[delta], rs.at[delta],
+            device_id=device(y, x + delta), device_id_type=MESH,
+        )
+        copies[delta].start()
+    parts = (own, one, two, three)
     for i, delta in enumerate(order):
         loads[i].wait()
-        if delta:
-            for copy in copies[delta]:
-                copy.wait()
+
+        def first(r, carry, i=i, delta=delta):
+            at = pl.ds(pl.multiple_of(r * BLK, BLK), BLK)
+            value = jnp.dot(parts[delta][at, :], wbuf[i, :FW, :], preferred_element_type=jnp.float32)
+            if i == 0:
+                value += jnp.dot(rest[0, at, :], wbuf[i, FW:, :], preferred_element_type=jnp.float32)
+            else:
+                value += total[at, :]
+            total[at, :] = value
+            return carry
+
+        lax.fori_loop(0, MOSTB, first, 0)
+    for i, delta in enumerate(order):
+        if delta == 0:
+            continue
+        copies[delta].wait()
 
         def rows(r, carry, i=i, delta=delta):
             at = pl.ds(pl.multiple_of(r * BLK, BLK), BLK)
-            value = jnp.dot(got[delta, at, :], wbuf[i], preferred_element_type=jnp.float32)
-            if i:
-                value += total[at, :]
+            value = total[at, :]
+            value += jnp.dot(got[delta, at, :], wbuf[i, FW:, :], preferred_element_type=jnp.float32)
             if i < SIDE - 1:
                 total[at, :] = value
             else:
@@ -363,67 +372,80 @@
         lax.fori_loop(0, MOSTB, rows, 0)
 
 
-def project(part, rest, w_out):
+def project(parts, rest, w_out):
     dma = pltpu.SemaphoreType.DMA
     vmem = pl.BlockSpec(memory_space=pltpu.VMEM)
     return pl.pallas_call(
         project_kernel,
         out_shape=jax.ShapeDtypeStruct((ROWS, D), jnp.bfloat16),
-        in_specs=[vmem, vmem, pl.BlockSpec(memory_space=pl.ANY)],
+        in_specs=[vmem] * 5 + [pl.BlockSpec(memory_space=pltpu.HBM)],
         out_specs=vmem,
         scratch_shapes=[
-            pltpu.VMEM((SIDE, ROWS, GW), jnp.bfloat16),
+            pltpu.VMEM((SIDE, ROWS, LW), jnp.bfloat16),
             pltpu.VMEM((SIDE, GW, D), jnp.bfloat16),
             pltpu.VMEM((ROWS, D), jnp.float32),
-            *[dma((SIDE,))] * 5,
+            *[dma((SIDE,))] * 3,
         ],
         compiler_params=pltpu.CompilerParams(
             collective_id=1, has_side_effects=True, vmem_limit_bytes=24 * 2**20
         ),
         name="project",
-    )(part, rest, w_out)
-
-
-def scatter_kernel(order, count, block, out):
-    live = pl.program_id(0) < count[lax.axis_index("frame")]
-
-    @pl.when(live)
-    def _():
-        out[...] = block[...]
-
-    @pl.when(jnp.logical_not(live))
-    def _():
-        out[...] = jnp.zeros_like(out)
-
-
-def scatter(order_row, count, normalized):
-    blocks = order_row.shape[1]
+    )(*parts, rest, w_out)
+
+
+def scatter_kernel(order, count, block, out, zero, sems):
+    own = count[lax.axis_index("frame")]
+    zero[...] = jnp.zeros_like(zero)
+
+    def each(act):
+        for j in range(order.shape[1]):
+            rows = pl.ds(pl.multiple_of(order[0, j] * BLK, BLK), BLK)
+            if j == MOSTB:
+                act(pltpu.make_async_copy(zero, out.at[rows, :], sems.at[j]))
+                continue
+
+            @pl.when(j < own)
+            def _(j=j, rows=rows):
+                act(pltpu.make_async_copy(block.at[pl.ds(j * BLK, BLK), :], out.at[rows, :], sems.at[j]))
+
+            @pl.when(j >= own)
+            def _(j=j, rows=rows):
+                act(pltpu.make_async_copy(zero, out.at[rows, :], sems.at[j]))
+
+    each(lambda copy: copy.start())
+    each(lambda copy: copy.wait())
+
+
+def scatter(keep_order, keep_count, normalized):
+    blocks = keep_order.shape[1]
+    smem = pl.BlockSpec(memory_space=pltpu.SMEM)
     return pl.pallas_call(
         scatter_kernel,
-        grid_spec=pltpu.PrefetchScalarGridSpec(
-            num_scalar_prefetch=2,
-            grid=(blocks,),
-            in_specs=[pl.BlockSpec((BLK, D), lambda j, order, count: (jnp.minimum(j, MOSTB - 1), 0))],
-            out_specs=pl.BlockSpec((BLK, D), lambda j, order, count: (order[0, j], 0)),
-        ),
+        in_specs=[smem, smem, pl.BlockSpec(memory_space=pltpu.VMEM)],
+        out_specs=pl.BlockSpec(memory_space=pl.ANY),
         out_shape=jax.ShapeDtypeStruct((blocks * BLK, D), jnp.bfloat16),
+        scratch_shapes=[pltpu.VMEM((BLK, D), jnp.bfloat16), pltpu.SemaphoreType.DMA((blocks,))],
+        compiler_params=pltpu.CompilerParams(vmem_limit_bytes=8 * 2**20),
         name="scatter",
-    )(order_row, count, normalized)
-
-
-def shifted(value, steps):
-    count = SIDE * SIDE
-    return lax.ppermute(value, "frame", [(f, (f + steps) % count) for f in range(count)])
+    )(keep_order, keep_count, normalized)
+
+
+def shifted(value, dy, dx):
+    def to(f):
+        return (f // SIDE + dy) % SIDE * SIDE + (f + dx) % SIDE
+
+    return lax.ppermute(value, "frame", [(f, to(f)) for f in range(SIDE * SIDE)])
 
 
 def shards(tokens, keep_count, keep_order, w_qkv, w_out):
     normed = norm_kept(keep_order, tokens)
     below, row, above, last, q = exchange(normed, w_qkv)
-    last_below = shifted(last, SIDE)
-    last_above = shifted(last, -SIDE)
+    last_below = shifted(last, 1, 0)
+    last_above = shifted(last, -1, 0)
     part = attend(0, 2, keep_count, q, below, row, above)
+    parts = [shifted(part[(SIDE - dx) % SIDE], 0, dx) if dx else part[0] for dx in range(SIDE)]
     rest = attend(2, 1, keep_count, q, last_below, last, last_above)
-    normalized = project(part, rest, w_out)
+    normalized = project(parts, rest, w_out)
     return scatter(keep_order, keep_count, normalized)
 
 

time: 126 us -> 112 us (0.89)
  the two profiles are of different devices: /device:TPU:120 before, /device:TPU:32 now
where the time goes in v4:
time: 112 us
  Pallas kernels  103 us (92%)
  starting transfers between devices  6.56 us (6%)
  local copies, waits for them, and re-layouts  2.14 us (2%)
    pallas_call x1, Pallas kernels, exchange(): pl.pallas_call(exchange_kernel, out_shape=[jax.ShapeDtypeStruct(shape, jn...  50.1 us
    pallas_call x2, Pallas kernels, attend(): pl.pallas_call(functools.partial(attend_kernel, start, pairs), out_shape=...  37.5 us
    pallas_call x1, Pallas kernels, project(): pl.pallas_call(project_kernel, out_shape=jax.ShapeDtypeStruct((ROWS, D),...  12.2 us
    ppermute x5, starting transfers between devices, shifted(): lax.ppermute(value, 'frame', [(f, to(f)) for f in range(SIDE * SIDE)])  6.56 us
  transfers between devices with their start and end apart: 5, of which 0 were waited for; matrix products, arithmetic and copies ran while one was open for 0% of the time, Pallas kernels for 33%

profile of v4, /device:TPU:32, one launch (start us, length us, event | category | flops | bytes accessed | tf_op | source)
XLA Modules:
  0.0 112.1 jit_solution(11503486656817321482)
XLA Ops:
  0.0 1.4 %copy-done = bf16[512,1536]{1,0:T(8,128)(2,1)S(1)} copy-done((bf16[512,1536]{1,0:T(8,128)(2,1)S(1)}, bf16[512,1536]{1,0:T(8,128)(2,1)}, u32[]{:S(2)}) %copy-start) | copy-done | bytes 1572888
  1.4 0.7 copy-done.1
  2.1 1.6 %norm_kept.1.normed = bf16[384,1536]{1,0:T(8,128)(2,1)S(1)} custom-call(s32[1,4]{1,0:T(1,128)S(1)} %copy-done.1, bf16[512,1536]{1,0:T(8,128)(2,1)S(1)} %copy-done), custom_call_target="tpu_custom_call" | custom-call | tf_op jit(solution)/shard_map/norm_kept/pallas_call | solution.py:48
  3.7 0.0 copy-start.3
  3.7 0.0 slice-start
  3.7 50.1 %exchange.1 = (bf16[4,384,512]{2,1,0:T(8,128)(2,1)S(1)}, bf16[4,384,512]{2,1,0:T(8,128)(2,1)S(1)}, bf16[4,384,512]{2,1,0:T(8,128)(2,1)S(1)}, bf16[4,384,256]{2,1,0:T(8,128)(2,1)S(1)}, bf16[4,384,384]{2,1,0:T(8,128)(2,1)S(1)}) custom-call(bf16[384,1536]{1,0:T(8,128)(2,1)S(1)} %norm_kept.1.normed, bf16[1536,4608]{1,0:T(8,128)(2,1)} %w.2), custom_call_target="tpu_custom_call" | custom-call | tf_op jit(solution)/shard_map/exchange/pallas_call | solution.py:151
  53.8 1.7 %collective-permute-start.4 = (bf16[4,384,256]{2,1,0:T(8,128)(2,1)S(1)}, bf16[4,384,256]{2,1,0:T(8,128)(2,1)S(1)}, u32[]{:S(2)}, u32[]{:S(2)}) collective-permute-start(bf16[4,384,256]{2,1,0:T(8,128)(2,1)S(1)} %get-tuple-element.14.row), channel_id=1, source_target_pairs={{0,96},{8,104},{16,112},{24,120},{32,0},{40,8},{48,16},{56,24},{64... | collective-permute-start | bytes 2359304 | tf_op jit(solution)/shard_map/ppermute | solution.py:437
  55.5 0.4 collective-permute-start.3
  55.9 0.0 copy-done.3
  55.9 23.9 %attend.2 = bf16[4,384,256]{2,1,0:T(8,128)(2,1)S(1)} custom-call(s32[16]{0:T(128)S(1)} %copy-done.3, bf16[4,384,384]{2,1,0:T(8,128)(2,1)S(1)} %get-tuple-element.10.q, bf16[4,384,512]{2,1,0:T(8,128)(2,1)S(1)} %get-tuple-element.11.below, bf16[4,384,512]{2,1,0:T(8,128)(2,1)S(1)} %get-tuple-element.12.row, bf16[4,384,512]{2,1,0:T(8,128)(2,1)S(1)} %get-tuple-element.13.above), custom_call_target="tpu_custom_call" | custom-call | flops 35999997952 | bytes 4194304 | tf_op jit(solution)/shard_map/attend/pallas_call | solution.py:299
  79.8 0.1 slice_bitcast_fusion
  79.9 3.0 %collective-permute-start.2 = (bf16[384,256]{1,0:T(8,128)(2,1)S(1)}, bf16[384,256]{1,0:T(8,128)(2,1)S(1)}, u32[]{:S(2)}, u32[]{:S(2)}) collective-permute-start(bf16[384,256]{1,0:T(8,128)(2,1)S(1)} %get-tuple-element.15), channel_id=1, source_target_pairs={{0,24},{8,0},{16,8},{24,16},{32,56},{40,32},{48,40},{56,48},{64,88... | collective-permute-start | bytes 589832 | tf_op jit(solution)/shard_map/ppermute | solution.py:437
  82.9 1.4 %collective-permute-start.1 = (bf16[384,256]{1,0:T(8,128)(2,1)S(1)}, bf16[384,256]{1,0:T(8,128)(2,1)S(1)}, u32[]{:S(2)}, u32[]{:S(2)}) collective-permute-start(bf16[384,256]{1,0:T(8,128)(2,1)S(1)} %get-tuple-element.16), channel_id=1, source_target_pairs={{0,16},{8,24},{16,0},{24,8},{32,48},{40,56},{48,32},{56,40},{64,80... | collective-permute-start | bytes 589832 | tf_op jit(solution)/shard_map/ppermute | solution.py:437
  84.3 0.0 collective-permute-start
  84.3 0.0 collective-permute-done.4.above
  84.3 0.0 collective-permute-done.3.below
  84.3 13.7 %attend.3.rest = bf16[4,384,128]{2,1,0:T(8,128)(2,1)S(1)} custom-call(s32[16]{0:T(128)S(1)} %copy-done.3, bf16[4,384,384]{2,1,0:T(8,128)(2,1)S(1)} %get-tuple-element.10.q, bf16[4,384,256]{2,1,0:T(8,128)(2,1)S(1)} %collective-permute-done.3.below, bf16[4,384,256]{2,1,0:T(8,128)(2,1)S(1)} %get-tuple-element.14.row, ...), custom_call_target="tpu_custom_call" | custom-call | flops 17999998976 | bytes 2097152 | tf_op jit(solution)/shard_map/attend/pallas_call | solution.py:299
  98.0 0.0 collective-permute-done.2.three
  98.0 0.0 collective-permute-done.1.two
  98.0 0.0 collective-permute-done.one
  98.0 0.0 slice-done
  98.1 0.0 copy-start.2
  98.1 12.2 %project.1.block = bf16[384,1536]{1,0:T(8,128)(2,1)S(1)} custom-call(bf16[384,256]{1,0:T(8,128)(2,1)S(1)} %get-tuple-element.18.own, bf16[384,256]{1,0:T(8,128)(2,1)S(1)} %collective-permute-done.one, bf16[384,256]{1,0:T(8,128)(2,1)S(1)} %collective-permute-done.1.two, bf16[384,256]{1,0:T(8,128)(2,1)S(1)} %collective-permute-done.2.three, ...), custom_call_target="tpu_custom_call" | custom-call | tf_op jit(solution)/shard_map/project/pallas_call | solution.py:378
  110.2 1.7 %scatter.1 = bf16[512,1536]{1,0:T(8,128)(2,1)} custom-call(s32[1,4]{1,0:T(1,128)S(1)} %copy-done.2, s32[16]{0:T(128)S(1)} %copy-done.3, bf16[384,1536]{1,0:T(8,128)(2,1)S(1)} %project.1.block), custom_call_target="tpu_custom_call" | custom-call | tf_op jit(solution)/shard_map/scatter/pallas_call | solution.py:422
  (6 shorter events, 0.0 us)
Async XLA Ops:
  0.0 1.4 %copy-start = (bf16[512,1536]{1,0:T(8,128)(2,1)S(1)}, bf16[512,1536]{1,0:T(8,128)(2,1)}, u32[]{:S(2)}) copy-start(bf16[512,1536]{1,0:T(8,128)(2,1)} %tokens.1) | copy-start | bytes 4718596
  1.4 0.7 copy-start.1
  3.7 52.2 %copy-start.3 = (s32[16]{0:T(128)S(1)}, s32[16]{0:T(128)}, u32[]{:S(2)}) copy-start(s32[16]{0:T(128)} %count.1) | copy-start | bytes 196
  3.7 94.3 %slice-start = ((s8[4718592]{0:T(1024)(128)(4,1)}), s8[4194304]{0:T(1024)(128)(4,1)S(1)}, s32[]{:S(2)}) async-start(s8[4718592]{0:T(1024)(128)(4,1)} %bitcast.8), calls=%async_computation | async-start | bytes 8388608
  53.8 30.5 %collective-permute-start.4 = (bf16[4,384,256]{2,1,0:T(8,128)(2,1)S(1)}, bf16[4,384,256]{2,1,0:T(8,128)(2,1)S(1)}, u32[]{:S(2)}, u32[]{:S(2)}) collective-permute-start(bf16[4,384,256]{2,1,0:T(8,128)(2,1)S(1)} %get-tuple-element.14.row), channel_id=1, source_target_pairs={{0,96},{8,104},{16,112},{24,120},{32,0},{40,8},{48,16},{56,24},{64... | collective-permute-start | bytes 2359304 | tf_op jit(solution)/shard_map/ppermute | solution.py:437
  55.5 28.8 %collective-permute-start.3 = (bf16[4,384,256]{2,1,0:T(8,128)(2,1)S(1)}, bf16[4,384,256]{2,1,0:T(8,128)(2,1)S(1)}, u32[]{:S(2)}, u32[]{:S(2)}) collective-permute-start(bf16[4,384,256]{2,1,0:T(8,128)(2,1)S(1)} %get-tuple-element.14.row), channel_id=1, source_target_pairs={{0,32},{8,40},{16,48},{24,56},{32,64},{40,72},{48,80},{56,88},{64,... | collective-permute-start | bytes 2359304 | tf_op jit(solution)/shard_map/ppermute | solution.py:437
  55.9 42.1 %slice-start.1 = ((s8[4718592]{0:T(1024)(128)(4,1)}), s8[524288]{0:T(1024)(128)(4,1)S(1)}, s32[]{:S(2)}) async-start(s8[4718592]{0:T(1024)(128)(4,1)} %bitcast.8), calls=%async_computation.1 | async-start | bytes 1048576
  79.9 18.1 %collective-permute-start.2 = (bf16[384,256]{1,0:T(8,128)(2,1)S(1)}, bf16[384,256]{1,0:T(8,128)(2,1)S(1)}, u32[]{:S(2)}, u32[]{:S(2)}) collective-permute-start(bf16[384,256]{1,0:T(8,128)(2,1)S(1)} %get-tuple-element.15), channel_id=1, source_target_pairs={{0,24},{8,0},{16,8},{24,16},{32,56},{40,32},{48,40},{56,48},{64,88... | collective-permute-start | bytes 589832 | tf_op jit(solution)/shard_map/ppermute | solution.py:437
  82.9 15.1 %collective-permute-start.1 = (bf16[384,256]{1,0:T(8,128)(2,1)S(1)}, bf16[384,256]{1,0:T(8,128)(2,1)S(1)}, u32[]{:S(2)}, u32[]{:S(2)}) collective-permute-start(bf16[384,256]{1,0:T(8,128)(2,1)S(1)} %get-tuple-element.16), channel_id=1, source_target_pairs={{0,16},{8,24},{16,0},{24,8},{32,48},{40,56},{48,32},{56,40},{64,80... | collective-permute-start | bytes 589832 | tf_op jit(solution)/shard_map/ppermute | solution.py:437
  84.3 13.7 %collective-permute-start = (bf16[384,256]{1,0:T(8,128)(2,1)S(1)}, bf16[384,256]{1,0:T(8,128)(2,1)S(1)}, u32[]{:S(2)}, u32[]{:S(2)}) collective-permute-start(bf16[384,256]{1,0:T(8,128)(2,1)S(1)} %get-tuple-element.17), channel_id=1, source_target_pairs={{0,8},{8,16},{16,24},{24,0},{32,40},{40,48},{48,56},{56,32},{64,72... | collective-permute-start | bytes 589832 | tf_op jit(solution)/shard_map/ppermute | solution.py:437
  98.1 12.2 %copy-start.2 = (s32[1,4]{1,0:T(1,128)S(1)}, s32[1,4]{1,0:T(1,128)}, u32[]{:S(2)}) copy-start(s32[1,4]{1,0:T(1,128)} %order.3) | copy-start | bytes 52
